TPU v7x, 128 devices: a whole 4x4x4 slice. The times are simulated.
128 devices in a mesh: stream: 8 (over y_hi, z), girth: 16 (over x, y_lo, core).
Axes of the slice: x: 4, y: 4 (y_hi: 2, y_lo: 2; y = y_hi * 2 + y_lo), z: 4, core: 2. Of those that a mesh axis runs over, the one named last changes fastest.
Arguments:
- velocity: float32 [3, 32, 128, 256], P(None, 'stream', 'girth'), may hold values from -6 to 6
- pressure: float32 [32, 128, 256], P('stream', 'girth'), may hold values from -6 to 6
- kinetic_energy: float32 [32, 128, 256], P('stream', 'girth'), may hold values from 0.01 to 1
- dissipation_rate: float32 [32, 128, 256], P('stream', 'girth'), may hold values from 0.5 to 20
- corner_ids: int32 [128, 1024], replicated, may hold values from 0 to 63230, as said below
- fractions: float32 [3, 128, 1024], replicated, may hold values from 0 to 1
- sector_owner: int32 [64, 1], replicated, may hold values from 0 to 15; in each aligned block of 64 rows (0 to 63, 64 to 127, ...) at most 12 rows name the same one
Outputs:
- new_velocity: float32 [3, 32, 128, 256], P(None, 'stream', 'girth')
- new_energy: float32 [32, 128, 256], P('stream', 'girth')
- new_rate: float32 [32, 128, 256], P('stream', 'girth')
- harmonics: float32 [128, 768], P(('stream', 'girth'))
Inputs may be any that keep to these rules, and one draw needn't show every extreme that they name: `corner_ids`: each entry is s * 8 * 256 + g * 256 + q with s from 0 to 30, g from 0 to 6 and q from 0 to 254. `sector_owner`: sector s covers azimuths s * 16 to (s + 1) * 16 - 1. Every girth index owns at least one sector and at most 12, and some girth index owns exactly 12.
All inputs are finite; a program needn't handle non-finite values.
Results may differ from a plain program's by a relative error of at most 0.000076.
Values sent between devices are 32-bit elements; how exact they have to be, the bound alone decides.
A program may use at most 192 MiB of HBM per device.

v0:
```python
import math

import jax
import jax.numpy as jnp
from jax import lax
from jax.sharding import PartitionSpec as P

NH = 128


base_viscosity = 0.05
time_step = 0.2
beta_star = 0.09
beta_rate = 0.075
alpha_rate = 0.52
wall_rate = 1.0


def extended_2(shard, sides, width):
    for axis, dim in sides:
        devices, length = (lax.axis_size(axis), shard.shape[dim])
        up = [(i, (i + 1) % devices) for i in range(devices - 1)]
        down = [(j, i) for i, j in up]
        last = lax.slice_in_dim(shard, length - width, length, axis=dim)
        leading = lax.slice_in_dim(shard, 0, width, axis=dim)
        before = lax.ppermute(last, axis, up)
        after = lax.ppermute(leading, axis, down)
        shard = jnp.concatenate([before, shard, after], axis=dim)
    return shard


def shifted(values, offsets):
    extent = values.shape
    return values[
        2 + offsets[0] : extent[0] - 2 + offsets[0],
        2 + offsets[1] : extent[1] - 2 + offsets[1],
        2 + offsets[2] : extent[2] - 2 + offsets[2],
    ]


def offset_of(direction, amount):
    offsets = [0, 0, 0]
    offsets[direction] = amount
    return tuple(offsets)


def derivative(values, direction):
    near_pair = shifted(values, offset_of(direction, 1)) - shifted(values, offset_of(direction, -1))
    far_pair = shifted(values, offset_of(direction, 2)) - shifted(values, offset_of(direction, -2))
    return (8.0 * near_pair - far_pair) / 12.0


def diffusion(values, viscosity, direction):
    center = shifted(values, (0, 0, 0))
    middle = shifted(viscosity, (0, 0, 0))
    upper_face = 0.5 * (middle + shifted(viscosity, offset_of(direction, 1)))
    lower_face = 0.5 * (middle + shifted(viscosity, offset_of(direction, -1)))
    return upper_face * (shifted(values, offset_of(direction, 1)) - center) - lower_face * (
        center - shifted(values, offset_of(direction, -1))
    )


def advance(padded):
    viscosity = base_viscosity + padded[4] / (padded[5] + wall_rate)
    centers = [shifted(padded[component], (0, 0, 0)) for component in range(6)]
    strain = jnp.zeros_like(centers[0])
    updated = []
    for component in range(3):
        change = -derivative(padded[3], component)
        for direction in range(3):
            gradient = derivative(padded[component], direction)
            strain = strain + gradient * gradient
            change = (
                change
                - centers[direction] * gradient
                + diffusion(padded[component], viscosity, direction)
            )
        updated.append(centers[component] + time_step * change)
    eddy_viscosity = centers[4] / (centers[5] + wall_rate)
    energy_change = eddy_viscosity * strain - beta_star * centers[4] * centers[5]
    rate_change = alpha_rate * strain - beta_rate * centers[5] * centers[5]
    for direction in range(3):
        energy_change = (
            energy_change
            - centers[direction] * derivative(padded[4], direction)
            + diffusion(padded[4], viscosity, direction)
        )
        rate_change = (
            rate_change
            - centers[direction] * derivative(padded[5], direction)
            + diffusion(padded[5], viscosity, direction)
        )
    return (
        jnp.stack(updated),
        centers[4] + time_step * energy_change,
        centers[5] + time_step * rate_change,
    )


def side_weight(fraction, upper_side):
    if upper_side:
        return fraction
    return 1.0 - fraction


def sample_points(
    flat_field,
    cell_ids,
    fracs,
    valid_cols,
    stream_first,
    cells_s,
    cells_g,
    cells_r,
    lowest_corner,
    highest_corner,
):
    plane_cells = cells_g * cells_r
    stream_cell = cell_ids // plane_cells
    remainder = cell_ids - stream_cell * plane_cells
    girth_cell = remainder // cells_r
    radial_cell = remainder - girth_cell * cells_r
    local_stream = stream_cell - stream_first
    counted = (local_stream >= lowest_corner) & (local_stream <= highest_corner)
    sampled = jnp.zeros((3,) + cell_ids.shape, jnp.float32)
    for along_s in (0, 1):
        for along_g in (0, 1):
            for along_r in (0, 1):
                weight = (
                    side_weight(fracs[0], along_s)
                    * side_weight(fracs[1], along_g)
                    * side_weight(fracs[2], along_r)
                )
                layer = local_stream + along_s
                inside = (layer >= 0) & (layer < cells_s) & counted & valid_cols[None, :]
                position = (
                    (jnp.clip(layer, 0, cells_s - 1) * cells_g + girth_cell + along_g) * cells_r
                    + radial_cell
                    + along_r
                )
                picked = jnp.take(flat_field, position.reshape(-1), axis=1).reshape(
                    (3,) + cell_ids.shape
                )
                sampled = sampled + jnp.where(inside, weight, 0.0) * picked
    return sampled


def fourier_table(azimuth_list, azimuths, modes):
    orders = lax.broadcasted_iota(jnp.int32, (1, modes), 1)
    phase_index = azimuth_list[:, None] * orders % azimuths
    angles = phase_index.astype(jnp.float32) * (2.0 * math.pi / azimuths)
    normalizer = 1.0 / math.sqrt(azimuths)
    return jnp.concatenate([jnp.cos(angles), -jnp.sin(angles)], axis=1) * normalizer


def body(velocity, pressure, kinetic_energy, dissipation_rate, corner_ids, fractions, sector_owner):
    stacked = jnp.concatenate(
        [velocity, pressure[None], kinetic_energy[None], dissipation_rate[None]], axis=0
    )
    extended = extended_2(stacked, (("stream", 1), ("girth", 2)), 2)
    padded = jnp.pad(extended, ((0, 0), (0, 0), (0, 0), (2, 2)))
    new_velocity, new_energy, new_rate = advance(padded)
    cells_s = velocity.shape[1]
    cells_g = velocity.shape[2]
    cells_r = velocity.shape[3]
    radii = corner_ids.shape[0]
    azimuths = corner_ids.shape[1]
    sectors = sector_owner.shape[0]
    width = azimuths // sectors
    girth_count = lax.axis_size("girth")
    stream_count = lax.axis_size("stream")
    girth_me = lax.axis_index("girth")
    stream_first = lax.axis_index("stream") * cells_s
    owners = sector_owner[:, 0]
    row_count = radii // (stream_count * girth_count)
    flat_field = new_velocity.reshape(3, -1)
    capacity = 3 * sectors // girth_count
    mine = (owners == girth_me).astype(jnp.int32)
    order = jnp.argsort(1 - mine, stable=True)[:capacity]
    live = mine[order]
    cell_ids = corner_ids.reshape(radii, sectors, width)[:, order].reshape(radii, capacity * width)
    fracs = fractions.reshape(3, radii, sectors, width)[:, :, order].reshape(
        3, radii, capacity * width
    )
    valid_cols = jnp.broadcast_to(live[:, None] > 0, (capacity, width)).reshape(-1)
    sector_pos = lax.broadcasted_iota(jnp.int32, (capacity, sectors), 1)
    chooser = ((order[:, None] == sector_pos) & (live[:, None] > 0)).astype(jnp.float32)
    sampled = sample_points(
        flat_field,
        cell_ids,
        fracs,
        valid_cols,
        stream_first,
        cells_s,
        cells_g,
        cells_r,
        -1,
        cells_s - 1,
    )
    spread = jnp.einsum(
        "crkw,ks->crsw",
        sampled.reshape(3, radii, capacity, width),
        chooser,
        precision=lax.Precision.HIGHEST,
    )
    disk = spread.reshape(3, radii, azimuths)
    own_rows = lax.psum_scatter(
        jnp.transpose(disk, (1, 0, 2)).reshape(
            row_count * lax.axis_size(("stream", "girth")), 3 * azimuths
        ),
        ("stream", "girth"),
        scatter_dimension=0,
        tiled=True,
    )
    full_table = fourier_table(lax.broadcasted_iota(jnp.int32, (azimuths,), 0), azimuths, NH)
    harmonics = jnp.dot(
        own_rows.reshape(row_count * 3, azimuths), full_table, precision=lax.Precision.HIGHEST
    ).reshape(row_count, 6 * NH)
    return (new_velocity, new_energy, new_rate, harmonics)


def solution(mesh):
    return jax.shard_map(
        body,
        mesh=mesh,
        in_specs=(
            P(None, "stream", "girth", None),
            P("stream", "girth", None),
            P("stream", "girth", None),
            P("stream", "girth", None),
            P(),
            P(),
            P(),
        ),
        out_specs=(
            P(None, "stream", "girth", None),
            P("stream", "girth", None),
            P("stream", "girth", None),
            P(("stream", "girth"), None),
        ),
        check_vma=False,
    )
```

profile of v0, /device:TPU:1, one launch (start us, length us, event | category | flops | bytes accessed | tf_op | source)
XLA Modules:
  0.0 1052.3 jit_solution(12667521340821685097)
XLA Ops:
  10.2 5.0 collective-permute-start
  17.1 2.0 sort.17
  21.8 1.9 copy.119
  26.1 2.9 collective-permute-start.3
  29.0 3.2 collective-permute-start.2
  36.5 2.9 copy.122
  39.3 84.0 %gather_fusion.10 = f32[24576,3]{1,0:T(8,128)} fusion(f32[3,8192]{0,1:T(8,128)} %copy.122, s32[24576]{0:T(1024)S(1)} %get-tuple-element.65), kind=kCustom, calls=%fused_computation.7.clone | custom fusion | bytes 688128 | tf_op jit(solution)/shard_map/jit(_take)/gather | solution.py:141
  123.4 14.7 %broadcast_select_fusion = f32[24576,3]{1,0:T(8,128)} fusion(f32[24576,3]{1,0:T(8,128)} %gather_fusion.10, pred[24576]{0:T(1024)(128)(4,1)S(1)} %get-tuple-element.72), kind=kLoop, calls=%fused_computation.11 | loop fusion | flops 73728 | bytes 614400 | tf_op jit(solution)/shard_map/jit(_take)/select_n | solution.py:141
  138.2 9.4 copy.145
  147.5 84.1 %gather_fusion.9 = f32[24576,3]{1,0:T(8,128)} fusion(f32[3,8192]{0,1:T(8,128)} %copy.122, s32[24576]{0:T(1024)S(1)} %get-tuple-element.64), kind=kCustom, calls=%fused_computation.6.clone | custom fusion | bytes 688128 | tf_op jit(solution)/shard_map/jit(_take)/gather | solution.py:141
  231.7 84.0 %gather_fusion.7 = f32[24576,3]{1,0:T(8,128)} fusion(f32[3,8192]{0,1:T(8,128)} %copy.122, s32[24576]{0:T(1024)S(1)} %get-tuple-element.62), kind=kCustom, calls=%fused_computation.4.clone | custom fusion | bytes 688128 | tf_op jit(solution)/shard_map/jit(_take)/gather | solution.py:141
  315.7 18.2 %broadcast_select_fusion.1 = (f32[24576,3]{1,0:T(8,128)}, f32[24576,3]{1,0:T(8,128)}) fusion(f32[24576,3]{1,0:T(8,128)} %gather_fusion.9, pred[24576]{0:T(1024)(128)(4,1)S(1)} %get-tuple-element.54, f32[24576,3]{1,0:T(8,128)} %gather_fusion.7, pred[24576]{0:T(1024)(128)(4,1)S(1)} %get-tuple-element.58), kind=kLoop, calls=%fused_computation.12 | loop fusion | flops 147456 | bytes 1228800 | tf_op jit(solution)/shard_map/jit(_take)/select_n | solution.py:141
  333.9 9.4 copy.142
  343.3 84.1 %gather_fusion.8 = f32[24576,3]{1,0:T(8,128)} fusion(f32[3,8192]{0,1:T(8,128)} %copy.122, s32[24576]{0:T(1024)S(1)} %get-tuple-element.63), kind=kCustom, calls=%fused_computation.5.clone | custom fusion | bytes 688128 | tf_op jit(solution)/shard_map/jit(_take)/gather | solution.py:141
  427.4 14.8 %broadcast_select_fusion.2 = f32[24576,3]{1,0:T(8,128)} fusion(f32[24576,3]{1,0:T(8,128)} %gather_fusion.8, pred[24576]{0:T(1024)(128)(4,1)S(1)} %get-tuple-element.73), kind=kLoop, calls=%fused_computation.13 | loop fusion | flops 73728 | bytes 614400 | tf_op jit(solution)/shard_map/jit(_take)/select_n | solution.py:141
  442.2 9.3 copy.139
  451.6 9.4 copy.136
  460.9 84.0 %gather_fusion.6 = f32[24576,3]{1,0:T(8,128)} fusion(f32[3,8192]{0,1:T(8,128)} %copy.122, s32[24576]{0:T(1024)S(1)} %get-tuple-element.61), kind=kCustom, calls=%fused_computation.3.clone | custom fusion | bytes 688128 | tf_op jit(solution)/shard_map/jit(_take)/gather | solution.py:141
  545.0 14.7 %broadcast_select_fusion.4 = f32[24576,3]{1,0:T(8,128)} fusion(f32[24576,3]{1,0:T(8,128)} %gather_fusion.6, pred[24576]{0:T(1024)(128)(4,1)S(1)} %get-tuple-element.74), kind=kLoop, calls=%fused_computation.15 | loop fusion | flops 73728 | bytes 614400 | tf_op jit(solution)/shard_map/jit(_take)/select_n | solution.py:141
  559.7 9.3 copy.133
  569.0 84.1 %gather_fusion.5 = f32[24576,3]{1,0:T(8,128)} fusion(f32[3,8192]{0,1:T(8,128)} %copy.122, s32[24576]{0:T(1024)S(1)} %get-tuple-element.60), kind=kCustom, calls=%fused_computation.2.clone | custom fusion | bytes 688128 | tf_op jit(solution)/shard_map/jit(_take)/gather | solution.py:141
  653.1 84.0 %gather_fusion.3 = f32[24576,3]{1,0:T(8,128)} fusion(f32[3,8192]{0,1:T(8,128)} %copy.122, s32[24576]{0:T(1024)S(1)} %get-tuple-element.52), kind=kCustom, calls=%fused_computation.clone | custom fusion | bytes 688128 | tf_op jit(solution)/shard_map/jit(_take)/gather | solution.py:141
  737.2 18.2 %broadcast_select_fusion.5 = (f32[24576,3]{1,0:T(8,128)}, f32[24576,3]{1,0:T(8,128)}) fusion(f32[24576,3]{1,0:T(8,128)} %gather_fusion.5, pred[24576]{0:T(1024)(128)(4,1)S(1)} %get-tuple-element.56, f32[24576,3]{1,0:T(8,128)} %gather_fusion.3, pred[24576]{0:T(1024)(128)(4,1)S(1)} %get-tuple-element.7), kind=kLoop, calls=%fused_computation.16 | loop fusion | flops 147456 | bytes 1228800 | tf_op jit(solution)/shard_map/jit(_take)/select_n | solution.py:141
  755.4 9.4 copy.130
  764.8 84.1 %gather_fusion.4 = f32[24576,3]{1,0:T(8,128)} fusion(f32[3,8192]{0,1:T(8,128)} %copy.122, s32[24576]{0:T(1024)S(1)} %get-tuple-element.53), kind=kCustom, calls=%fused_computation.1.clone | custom fusion | bytes 688128 | tf_op jit(solution)/shard_map/jit(_take)/gather | solution.py:141
  848.9 15.0 %broadcast_select_fusion.6 = f32[24576,3]{1,0:T(8,128)} fusion(f32[24576,3]{1,0:T(8,128)} %gather_fusion.4, pred[24576]{0:T(1024)(128)(4,1)S(1)} %copy-done.12), kind=kLoop, calls=%fused_computation.17 | loop fusion | flops 73728 | bytes 614400 | tf_op jit(solution)/shard_map/jit(_take)/select_n | solution.py:141
  863.9 9.3 copy.127
  873.3 10.0 copy.124
  885.6 2.1 copy.147
  887.7 2.1 sine_negate_fusion
  892.9 149.1 %all-reduce.4.cloned.1.call-done = f32[128,3072]{0,1:T(8,128)} async-done(((f32[128,3072]{0,1:T(8,128)}), f32[128,3072]{0,1:T(8,128)}) %all-reduce.4.cloned.1.call-update) | async-done | bytes 1572880
  1042.0 2.3 dynamic-slice_reduce_fusion
  (75 shorter events, 20.6 us)
Async XLA Ops:
  7.2 18.8 %copy-start.6 = (f32[4,8,256]{2,1,0:T(8,128)S(1)}, f32[4,8,256]{2,1,0:T(8,128)}, u32[]{:S(2)}) copy-start(f32[4,8,256]{2,1,0:T(8,128)} %param.12) | copy-start | bytes 98308
  7.2 18.8 %copy-start.7 = (f32[4,8,256]{2,1,0:T(8,128)S(1)}, f32[4,8,256]{2,1,0:T(8,128)}, u32[]{:S(2)}) copy-start(f32[4,8,256]{2,1,0:T(8,128)} %param.11) | copy-start | bytes 98308
  7.2 18.8 %copy-start.8 = (f32[4,8,256]{2,1,0:T(8,128)S(1)}, f32[4,8,256]{2,1,0:T(8,128)}, u32[]{:S(2)}) copy-start(f32[4,8,256]{2,1,0:T(8,128)} %param.10) | copy-start | bytes 98308
  7.2 18.8 %copy-start = (f32[3,4,8,256]{3,2,1,0:T(8,128)S(1)}, f32[3,4,8,256]{3,2,1,0:T(8,128)}, u32[]{:S(2)}) copy-start(f32[3,4,8,256]{3,2,1,0:T(8,128)} %param.9) | copy-start | bytes 294916
  7.2 1034.8 %all-reduce.4.cloned.1.call-start = ((), (), s32[]{:S(2)}) async-start(), calls=%async_computation | async-start | bytes 3145728
  8.9 17.1 %collective-permute-start.1 = (f32[6,2,8,256]{3,2,1,0:T(8,128)}, f32[6,2,8,256]{3,2,1,0:T(8,128)S(1)}, u32[]{:S(2)}, u32[]{:S(2)}) collective-permute-start(f32[6,2,8,256]{3,2,1,0:T(8,128)} %get-tuple-element.51), channel_id=1, source_target_pairs={{16,0},{32,16},{48,32},{64,48},{80,64},{96,80},{112,96},{17,1},{33... | collective-permute-start | bytes 294920 | tf_op jit(solution)/shard_map/ppermute | solution.py:27
  10.2 15.8 %collective-permute-start = (f32[6,2,8,256]{3,2,1,0:T(8,128)S(1)}, f32[6,2,8,256]{3,2,1,0:T(8,128)S(1)}, u32[]{:S(2)}, u32[]{:S(2)}) collective-permute-start(f32[6,2,8,256]{3,2,1,0:T(8,128)S(1)} %get-tuple-element.50), channel_id=1, source_target_pairs={{0,16},{16,32},{32,48},{48,64},{64,80},{80,96},{96,112},{1,17},{17... | collective-permute-start | bytes 294920 | tf_op jit(solution)/shard_map/ppermute | solution.py:26
  26.1 6.9 collective-permute-start.3
  29.0 4.8 collective-permute-start.2
  35.6 102.5 %copy-start.1 = (f32[4,8,256]{2,1,0:T(8,128)}, f32[4,8,256]{2,1,0:T(8,128)S(1)}, u32[]{:S(2)}) copy-start(f32[4,8,256]{2,1,0:T(8,128)S(1)} %get-tuple-element.27) | copy-start | bytes 98308
  35.6 102.5 %copy-start.2 = (f32[4,8,256]{2,1,0:T(8,128)}, f32[4,8,256]{2,1,0:T(8,128)S(1)}, u32[]{:S(2)}) copy-start(f32[4,8,256]{2,1,0:T(8,128)S(1)} %get-tuple-element.29) | copy-start | bytes 98308
  35.6 102.5 %copy-start.3 = (f32[4,8,256]{2,1,0:T(8,128)}, f32[4,8,256]{2,1,0:T(8,128)S(1)}, u32[]{:S(2)}) copy-start(f32[4,8,256]{2,1,0:T(8,128)S(1)} %get-tuple-element.30) | copy-start | bytes 98308
  35.6 102.5 %copy-start.4 = (f32[4,8,256]{2,1,0:T(8,128)}, f32[4,8,256]{2,1,0:T(8,128)S(1)}, u32[]{:S(2)}) copy-start(f32[4,8,256]{2,1,0:T(8,128)S(1)} %get-tuple-element.32) | copy-start | bytes 98308
  35.6 102.5 %copy-start.5 = (f32[4,8,256]{2,1,0:T(8,128)}, f32[4,8,256]{2,1,0:T(8,128)S(1)}, u32[]{:S(2)}) copy-start(f32[4,8,256]{2,1,0:T(8,128)S(1)} %get-tuple-element.33) | copy-start | bytes 98308
  35.8 102.3 %copy-start.9 = (f32[4,8,256]{2,1,0:T(8,128)}, f32[4,8,256]{2,1,0:T(8,128)S(1)}, u32[]{:S(2)}) copy-start(f32[4,8,256]{2,1,0:T(8,128)S(1)} %fusion.84) | copy-start | bytes 98308
  36.1 102.1 %copy-start.10 = (f32[4,8,256]{2,1,0:T(8,128)}, f32[4,8,256]{2,1,0:T(8,128)S(1)}, u32[]{:S(2)}) copy-start(f32[4,8,256]{2,1,0:T(8,128)S(1)} %fusion.102) | copy-start | bytes 98308
  36.3 101.8 %copy-start.11 = (f32[4,8,256]{2,1,0:T(8,128)}, f32[4,8,256]{2,1,0:T(8,128)S(1)}, u32[]{:S(2)}) copy-start(f32[4,8,256]{2,1,0:T(8,128)S(1)} %fusion.126) | copy-start | bytes 98308
  755.4 93.5 %copy-start.12 = (pred[24576]{0:T(1024)(128)(4,1)S(1)}, pred[24576]{0:T(1024)(128)(4,1)}, u32[]{:S(2)}) copy-start(pred[24576]{0:T(1024)(128)(4,1)} %get-tuple-element.75) | copy-start | bytes 73732
Sparse Core Ops, SparseCore 0:
  887.8 154.1 all-reduce.3
where the time goes:
time: 1050 us
  local copies, waits for them, and re-layouts  763 us (73%)
  waiting for transfers between devices  150 us (14%)
  other arithmetic  111 us (11%)
  between operations  14.5 us (1%)
  starting transfers between devices  12.4 us (1%)
    gather x8, local copies, waits for them, and re-layouts, sample_points(): jnp.take(flat_field, position.reshape(-1), axis=1)  673 us
    unnamed x2, waiting for transfers between devices  149 us
    select_n x6, other arithmetic, sample_points(): jnp.take(flat_field, position.reshape(-1), axis=1)  95.7 us
    reshape x8, local copies, waits for them, and re-layouts, sample_points(): jnp.take(flat_field, position.reshape(-1), axis=1)  75.5 us
  transfers between devices with their start and end apart: 5, of which 2 were waited for; matrix products, arithmetic and copies ran while one was open for 2% of the time, Pallas kernels for 0%

commit v1 on v0

v1 whole, which is shorter than its diff:
```python
import functools
import math

import jax
import jax.numpy as jnp
import numpy as np
from jax import lax
from jax.experimental import pallas as pl
from jax.experimental.pallas import tpu as pltpu
from jax.sharding import PartitionSpec as P

F32 = jnp.float32
BF16 = jnp.bfloat16
MESH = pl.DeviceIdType.MESH

base_viscosity = 0.05
time_step = 0.2
beta_star = 0.09
beta_rate = 0.075
alpha_rate = 0.52
wall_rate = 1.0

STREAM = 8
GIRTH = 16
RING = 4
PLANE = 32
CELLS_S = 4
CELLS_G = 8
CELLS_R = 256
AZIMUTHS = 1024
MODES = 128
SECTORS = 64
WIDTH = 16
ROWS = 3 * CELLS_S * CELLS_G
TILES = 24


def fourier_parts():
    a = np.arange(AZIMUTHS)[:, None]
    h = np.arange(MODES)[None, :]
    angle = (a * h % AZIMUTHS) * (2.0 * math.pi / AZIMUTHS)
    table = np.concatenate([np.cos(angle), -np.sin(angle)], axis=1) / math.sqrt(AZIMUTHS)
    table = table.astype(np.float32)
    high = table.astype(jnp.bfloat16)
    low = (table - high.astype(np.float32)).astype(jnp.bfloat16)
    return np.concatenate([high, low], axis=1)


def parts_of(x, count):
    parts = []
    for _ in range(count):
        part = x.astype(BF16)
        parts.append(part)
        x = x - part.astype(F32)
    return parts


def slope(up1, down1, up2, down2):
    return (8.0 * (up1 - down1) - (up2 - down2)) * (1.0 / 12.0)


def viscosity_of(energy, rate):
    return base_viscosity + energy / (rate + wall_rate)


def lane_shift(x, amount, fill):
    lane = lax.broadcasted_iota(jnp.int32, x.shape, 1)
    rolled = pltpu.roll(x, (-amount) % CELLS_R, axis=1)
    inside = (lane + amount >= 0) & (lane + amount < CELLS_R)
    return jnp.where(inside, rolled, fill)


def flux(center, up, down, v, v_up, v_down):
    return 0.5 * (v + v_up) * (up - center) - 0.5 * (v + v_down) * (center - down)


def stencil_layer(cells, above, wide, s):
    def at(f, ds, dg):
        if dg != 0:
            return wide[f, s, 8 + dg : 16 + dg, :]
        if s + ds < 0:
            return above[0, f, 2 + s + ds]
        if s + ds >= CELLS_S:
            return above[1, f, s + ds - CELLS_S]
        return cells[f, s + ds]

    v = viscosity_of(at(4, 0, 0), at(5, 0, 0))
    v_side = [
        [viscosity_of(at(4, d, 0), at(5, d, 0)) for d in (1, -1)],
        [viscosity_of(at(4, 0, d), at(5, 0, d)) for d in (1, -1)],
        [lane_shift(v, d, base_viscosity) for d in (1, -1)],
    ]
    centers = [at(f, 0, 0) for f in range(6)]

    def around(f, d):
        if d == 0:
            return [at(f, j, 0) for j in (1, -1, 2, -2)]
        if d == 1:
            return [at(f, 0, j) for j in (1, -1, 2, -2)]
        return [lane_shift(centers[f], j, 0.0) for j in (1, -1, 2, -2)]

    strain = None
    updated = []
    for c in range(3):
        change = -slope(*around(3, c))
        for d in range(3):
            near = around(c, d)
            gradient = slope(*near)
            square = gradient * gradient
            strain = square if strain is None else strain + square
            change = change - centers[d] * gradient
            change = change + flux(centers[c], near[0], near[1], v, *v_side[d])
        updated.append(centers[c] + time_step * change)
    eddy = centers[4] / (centers[5] + wall_rate)
    changes = [
        eddy * strain - beta_star * centers[4] * centers[5],
        alpha_rate * strain - beta_rate * centers[5] * centers[5],
    ]
    for i, f in enumerate((4, 5)):
        change = changes[i]
        for d in range(3):
            near = around(f, d)
            change = change - centers[d] * slope(*near)
            change = change + flux(centers[f], near[0], near[1], v, *v_side[d])
        updated.append(centers[f] + time_step * change)
    return updated


def point_tiles(a):
    lane = lax.broadcasted_iota(jnp.int32, (16, 128), 1)
    first = jnp.concatenate([a[0:16, 0:128], a[16:32, 0:128]], axis=1)
    rest = jnp.where(lane < 64, a[0:16, 128:256], a[16:32, 128:256])
    rest = jnp.concatenate([rest[0:8], rest[8:16]], axis=1)
    return jnp.concatenate([first, rest], axis=0)


def radius_rows(d):
    lane = lax.broadcasted_iota(jnp.int32, (16, 128), 1)
    first = jnp.concatenate([d[0:16, 0:128], d[0:16, 128:256]], axis=0)
    rest = jnp.concatenate([d[16:24, 0:128], d[16:24, 128:256]], axis=0)
    low = jnp.where(lane < 64, rest, 0.0)
    high = jnp.where(lane < 64, 0.0, rest)
    return jnp.concatenate([first, jnp.concatenate([low, high], axis=0)], axis=1)


def kernel(
    vel, pre, kin, dis, ids, frac, owner, ftab,
    nv_o, ne_o, nr_o, harm_o,
    cells, above, wide, pack, edge, nv, ids_v, frac_v, ft, choose, W, lhs, vec, acc, disk, four, sendb, recvb,
    in_sem, hs_sem, hr_sem, gs_sem, gr_sem, as_sem, ar_sem,
):
    t = lax.axis_index("stream")
    g = lax.axis_index("girth")
    y = t // RING
    z = lax.rem(t, RING)
    me = y * GIRTH + g

    own = [
        pltpu.make_async_copy(vel, cells.at[0:3], in_sem.at[0]),
        pltpu.make_async_copy(pre, cells.at[3], in_sem.at[1]),
        pltpu.make_async_copy(kin, cells.at[4], in_sem.at[2]),
        pltpu.make_async_copy(dis, cells.at[5], in_sem.at[3]),
    ]
    points = []
    for half in range(2):
        rows = pl.ds((half * RING + z) * GIRTH, GIRTH)
        points.append(
            pltpu.make_async_copy(ids.at[rows, :], ids_v.at[half], in_sem.at[4 + half])
        )
        points.append(
            pltpu.make_async_copy(frac.at[:, rows, :], frac_v.at[half], in_sem.at[6 + half])
        )
    points.append(pltpu.make_async_copy(ftab, ft, in_sem.at[8]))
    for copy in own + points:
        copy.start()

    barrier = pltpu.get_barrier_semaphore()

    def plane_peer(i):
        other = lax.rem(me + i, PLANE)
        return other, (other // GIRTH * RING + z, lax.rem(other, GIRTH))

    def ring_peer(i):
        return (y * RING + lax.rem(z + i, RING), g)

    def greet(i, carry):
        pl.semaphore_signal(barrier, inc=1, device_id=plane_peer(i)[1], device_id_type=MESH)
        return carry

    for i in range(1, RING):
        pl.semaphore_signal(barrier, inc=1, device_id=ring_peer(i), device_id_type=MESH)
    seam_up = t == RING - 1
    seam_down = t == RING

    @pl.when(seam_up)
    def _():
        pl.semaphore_signal(barrier, inc=1, device_id=(t + 1, g), device_id_type=MESH)

    @pl.when(seam_down)
    def _():
        pl.semaphore_signal(barrier, inc=1, device_id=(t - 1, g), device_id_type=MESH)

    lax.fori_loop(1, PLANE, greet, 0)

    for copy in own:
        copy.wait()
    for f in range(6):
        for s in range(CELLS_S):
            pack[0, f, 2 * s : 2 * s + 2, :] = cells[f, s, 0:2, :]
            pack[1, f, 2 * s : 2 * s + 2, :] = cells[f, s, 6:8, :]
            wide[f, s, 8:16, :] = cells[f, s]

    seam = jnp.where(seam_up | seam_down, 1, 0)
    pl.semaphore_wait(barrier, PLANE - 1 + RING - 1 + seam)

    def halo(k):
        if k == 0:
            src, dst, dev = cells.at[:, 0:2], above.at[1], (t - 1, g)
        elif k == 1:
            src, dst, dev = cells.at[:, 2:4], above.at[0], (t + 1, g)
        elif k == 2:
            src, dst, dev = pack.at[0], edge.at[1], (t, g - 1)
        else:
            src, dst, dev = pack.at[1], edge.at[0], (t, g + 1)
        return pltpu.make_async_remote_copy(
            src_ref=src, dst_ref=dst, send_sem=hs_sem.at[k], recv_sem=hr_sem.at[k],
            device_id=dev, device_id_type=MESH,
        )

    sends = (t > 0, t < STREAM - 1, g > 0, g < GIRTH - 1)
    receives = (sends[1], sends[0], sends[3], sends[2])
    for k in range(4):
        pl.when(sends[k])(lambda k=k: halo(k).start())

    @pl.when(t == 0)
    def _():
        above[0] = jnp.zeros((6, 2, 8, CELLS_R), F32)

    @pl.when(t == STREAM - 1)
    def _():
        above[1] = jnp.zeros((6, 2, 8, CELLS_R), F32)

    @pl.when(g == 0)
    def _():
        edge[0] = jnp.zeros((6, 8, CELLS_R), F32)

    @pl.when(g == GIRTH - 1)
    def _():
        edge[1] = jnp.zeros((6, 8, CELLS_R), F32)

    sub8 = lax.broadcasted_iota(jnp.int32, (8, 128), 0)
    lane8 = lax.broadcasted_iota(jnp.int32, (8, 128), 1)

    def sector(s, carry):
        count, place = carry
        mine = jnp.where(owner[s, 0] == g, 1, 0)
        here = (sub8 == s // 8) & (lane8 // WIDTH == lax.rem(s, 8))
        value = jnp.where(mine > 0, count * WIDTH, -AZIMUTHS) + lax.rem(lane8, WIDTH)
        return count + mine, jnp.where(here, value, place)

    _, place = lax.fori_loop(
        0, SECTORS, sector, (jnp.int32(0), jnp.full((8, 128), -AZIMUTHS, jnp.int32))
    )
    row = lax.broadcasted_iota(jnp.int32, (256, 128), 0)
    slot = jnp.where(row < 192, row, row - 64)
    for k in range(8):
        hit = slot == place[k : k + 1, :]
        choose[:, k * 128 : (k + 1) * 128] = jnp.where(hit, 1.0, 0.0).astype(BF16)

    for copy in points:
        copy.wait()
    cid = ids_v[...].reshape(PLANE, AZIMUTHS)
    stream_cell = lax.shift_right_logical(cid, 11)
    girth_cell = lax.shift_right_logical(cid, 8) & 7
    wall_cell = cid & 255
    stack = [wall_cell.astype(F32).astype(BF16), stream_cell.astype(F32).astype(BF16)]
    stack.append(girth_cell.astype(F32).astype(BF16))
    for i in range(3):
        stack.extend(parts_of(frac_v[:, i].reshape(PLANE, AZIMUTHS), 3))
    picked = lax.dot_general(
        jnp.concatenate(stack, axis=0), choose[...], (((1,), (1,)), ((), ())),
        preferred_element_type=F32,
    )
    part = [picked[32 * i : 32 * i + 32] for i in range(12)]
    cell_q, cell_s, cell_g = [point_tiles(part[i]) for i in range(3)]
    f_s, f_g, f_q = [
        point_tiles(part[3 + 3 * i] + part[4 + 3 * i] + part[5 + 3 * i]) for i in range(3)
    ]
    vec[0] = cell_s
    vec[1] = f_s
    vec[2] = cell_g
    vec[3] = f_g
    vec[4] = cell_q
    low_parts = parts_of(1.0 - f_q, 2)
    high_parts = parts_of(f_q, 2)
    vec[5] = low_parts[0].astype(F32)
    vec[6] = low_parts[1].astype(F32)
    vec[7] = high_parts[0].astype(F32)
    vec[8] = high_parts[1].astype(F32)

    chosen = jnp.dot(choose[...], ft[...], preferred_element_type=F32).astype(BF16)
    four[0:256, :] = chosen[:, 0:256]
    four[256:512, :] = chosen[:, 0:256]
    four[512:768, :] = chosen[:, 256:512]

    def weights(n, carry):
        def v(i):
            return vec[i, pl.ds(n, 1), :]

        q = lax.broadcasted_iota(jnp.int32, (CELLS_R, 256), 0).astype(F32)
        at_q = q == v(4)
        at_up = q == v(4) + 1.0
        high = jnp.where(at_q, v(5), jnp.where(at_up, v(7), 0.0)).astype(BF16)
        low = jnp.where(at_q, v(6), jnp.where(at_up, v(8), 0.0)).astype(BF16)
        cols = pl.ds(pl.multiple_of(n * 256, 256), 256)
        W[0:256, cols] = high
        W[256:512, cols] = high
        W[512:768, cols] = low
        return carry

    lax.fori_loop(0, TILES, weights, 0)
    sendb[...] = jnp.zeros_like(sendb)

    for k in range(4):
        pl.when(receives[k])(lambda k=k: halo(k).wait_recv())
    for f in range(6):
        for s in range(CELLS_S):
            wide[f, s, 6:8, :] = edge[0, f, 2 * s : 2 * s + 2, :]
            wide[f, s, 16:18, :] = edge[1, f, 2 * s : 2 * s + 2, :]
    for s in range(CELLS_S):
        updated = stencil_layer(cells, above, wide, s)
        for c in range(3):
            nv[0, c * 32 + s * 8 : c * 32 + s * 8 + 8, :] = updated[c]
        ne_o[s] = updated[3]
        nr_o[s] = updated[4]

    def gather(i):
        return pltpu.make_async_remote_copy(
            src_ref=nv.at[0], dst_ref=nv.at[RING - i], send_sem=gs_sem.at[i], recv_sem=gr_sem.at[i],
            device_id=ring_peer(i), device_id_type=MESH,
        )

    def gathered(i):
        return gather(RING - i)

    for i in (1, 3, 2):
        gather(i).start()
    for c in range(3):
        for s in range(CELLS_S):
            nv_o[c, s] = nv[0, c * 32 + s * 8 : c * 32 + s * 8 + 8, :]

    def load_block(i):
        high, low = parts_of(nv[i], 2)
        lhs[i * ROWS : (i + 1) * ROWS, :] = jnp.concatenate([high, low, high], axis=1)

    def layers(blocks, n, sums):
        first, count = blocks
        cols = pl.ds(pl.multiple_of(n * 256, 256), 256)
        out = jnp.dot(
            lhs[first * ROWS : (first + count) * ROWS, :], W[:, cols],
            preferred_element_type=F32,
        )
        cell = jnp.broadcast_to(vec[0, pl.ds(n, 1), :], (8, 256))
        up = jnp.broadcast_to(vec[1, pl.ds(n, 1), :], (8, 256))
        stay = 1.0 - up
        for b in range(count):
            base = ((y * RING + lax.rem(z + first + b, RING)) * CELLS_S).astype(F32)
            above = cell - base
            for s in range(CELLS_S):
                weight = jnp.where(above == s, stay, jnp.where(above == s - 1, up, 0.0))
                for c in range(3):
                    at = b * ROWS + c * 32 + s * 8
                    term = weight * out[at : at + 8]
                    sums[c] = term if sums[c] is None else sums[c] + term
        return sums

    load_block(0)

    def first_pass(n, carry):
        sums = layers((0, 1), n, [None] * 3)
        for c in range(3):
            acc[c * TILES + n] = sums[c]
        return carry

    lax.fori_loop(0, TILES, first_pass, 0)

    for i in (1, 3, 2):
        gathered(i).wait_recv()
        load_block(i)

    def second_pass(n, carry):
        sums = layers((1, 3), n, [acc[c * TILES + n] for c in range(3)])
        cell = vec[2, pl.ds(n, 1), :]
        up = vec[3, pl.ds(n, 1), :]
        side = lax.broadcasted_iota(jnp.int32, (8, 256), 0).astype(F32)
        weight = jnp.where(side == cell, 1.0 - up, jnp.where(side == cell + 1.0, up, 0.0))
        for c in range(3):
            disk[pl.ds(c * TILES + n, 1), :] = jnp.sum(sums[c] * weight, axis=0, keepdims=True)
        return carry

    lax.fori_loop(0, TILES, second_pass, 0)

    rows = jnp.concatenate(
        [radius_rows(disk[c * TILES : (c + 1) * TILES, :]) for c in range(3)], axis=0
    )
    high, low = parts_of(rows, 2)
    spectrum = jnp.dot(
        jnp.concatenate([high, low, high], axis=1), four[...], preferred_element_type=F32
    )
    for c in range(3):
        for k in range(2):
            sendb[pl.ds(2 * c + k, PLANE, stride=8), :] = spectrum[
                c * PLANE : (c + 1) * PLANE, k * 128 : (k + 1) * 128
            ]

    def slot_of(i):
        return pl.ds(pl.multiple_of(i * 8, 8), 8)

    def post(i):
        other, dev = plane_peer(i)
        return pltpu.make_async_remote_copy(
            src_ref=sendb.at[slot_of(other), :], dst_ref=recvb.at[slot_of(i), :],
            send_sem=as_sem.at[i], recv_sem=ar_sem.at[i], device_id=dev, device_id_type=MESH,
        )

    def post_one(i, carry):
        post(i).start()
        return carry

    lax.fori_loop(1, PLANE, post_one, 0)

    def take_one(i, carry):
        post(i).wait_recv()
        return carry

    lax.fori_loop(1, PLANE, take_one, 0)
    total = sendb[slot_of(me), :]
    for i in range(1, PLANE):
        total = total + recvb[8 * i : 8 * i + 8, :]
    for k in range(6):
        harm_o[0:1, k * 128 : (k + 1) * 128] = total[k : k + 1, :]

    for k in range(4):
        pl.when(sends[k])(lambda k=k: halo(k).wait_send())
    for i in range(1, RING):
        gather(i).wait_send()

    def sent_one(i, carry):
        post(i).wait_send()
        return carry

    lax.fori_loop(1, PLANE, sent_one, 0)


def body(velocity, pressure, kinetic_energy, dissipation_rate, corner_ids, fractions, sector_owner):
    hbm = pl.BlockSpec(memory_space=pltpu.HBM)
    vmem = pl.BlockSpec(memory_space=pltpu.VMEM)
    smem = pl.BlockSpec(memory_space=pltpu.SMEM)
    dma = pltpu.SemaphoreType.DMA
    return pl.pallas_call(
        kernel,
        out_shape=(
            jax.ShapeDtypeStruct(velocity.shape, F32),
            jax.ShapeDtypeStruct(pressure.shape, F32),
            jax.ShapeDtypeStruct(pressure.shape, F32),
            jax.ShapeDtypeStruct((1, 6 * MODES), F32),
        ),
        in_specs=[hbm] * 6 + [smem, hbm],
        out_specs=(vmem,) * 4,
        scratch_shapes=[
            pltpu.VMEM((6, CELLS_S, CELLS_G, CELLS_R), F32),
            pltpu.VMEM((2, 6, 2, CELLS_G, CELLS_R), F32),
            pltpu.VMEM((6, CELLS_S, 24, CELLS_R), F32),
            pltpu.VMEM((2, 6, 8, CELLS_R), F32),
            pltpu.VMEM((2, 6, 8, CELLS_R), F32),
            pltpu.VMEM((RING, ROWS, CELLS_R), F32),
            pltpu.VMEM((2, GIRTH, AZIMUTHS), jnp.int32),
            pltpu.VMEM((2, 3, GIRTH, AZIMUTHS), F32),
            pltpu.VMEM((AZIMUTHS, 512), BF16),
            pltpu.VMEM((256, AZIMUTHS), BF16),
            pltpu.VMEM((768, TILES * 256), BF16),
            pltpu.VMEM((RING * ROWS, 768), BF16),
            pltpu.VMEM((9, TILES, 256), F32),
            pltpu.VMEM((3 * TILES, 8, 256), F32),
            pltpu.VMEM((3 * TILES, 256), F32),
            pltpu.VMEM((768, 256), BF16),
            pltpu.VMEM((PLANE * 8, 128), F32),
            pltpu.VMEM((PLANE * 8, 128), F32),
            dma((9,)),
            dma((4,)),
            dma((4,)),
            dma((RING,)),
            dma((RING,)),
            dma((PLANE,)),
            dma((PLANE,)),
        ],
        compiler_params=pltpu.CompilerParams(
            collective_id=0, has_side_effects=True, vmem_limit_bytes=48 * 1024 * 1024
        ),
    )(
        velocity, pressure, kinetic_energy, dissipation_rate, corner_ids, fractions, sector_owner,
        jnp.asarray(fourier_parts()),
    )


def solution(mesh):
    return jax.shard_map(
        body,
        mesh=mesh,
        in_specs=(
            P(None, "stream", "girth", None),
            P("stream", "girth", None),
            P("stream", "girth", None),
            P("stream", "girth", None),
            P(),
            P(),
            P(),
        ),
        out_specs=(
            P(None, "stream", "girth", None),
            P("stream", "girth", None),
            P("stream", "girth", None),
            P(("stream", "girth"), None),
        ),
        check_vma=False,
    )
```

time: 1050 us -> 48.2 us (0.05)
  local copies, waits for them, and re-layouts: 763 us -> 10 us
  waiting for transfers between devices: 150 us -> 0 us
  other arithmetic: 111 us -> 0 us
  Pallas kernels: 0 us -> 37.1 us
  between operations: 14.5 us -> 0.65 us
  starting transfers between devices: 12.4 us -> 0 us
    gather x13 -> x0, local copies, waits for them, and re-layouts: 675 us -> none  [the longest x8 673 us: sample_points(): jnp.take(flat_field, position.reshape(-1), axis=1)]
    unnamed x2 -> x0, waiting for transfers between devices: 149 us -> none
    select_n x8 -> x0, other arithmetic: 97.5 us -> none  [the longest x6 95.7 us: sample_points(): jnp.take(flat_field, position.reshape(-1), axis=1)]
    reshape x10 -> x0, local copies, waits for them, and re-layouts: 75.8 us -> none  [the longest x8 75.5 us: sample_points(): jnp.take(flat_field, position.reshape(-1), axis=1)]
    pallas_call x0 -> x1, Pallas kernels: none -> 37.1 us  [body(): pl.pallas_call(kernel, out_shape=(jax.ShapeDtypeStruct(velocity.shape, F3...]
    ppermute x4 -> x0, starting transfers between devices: 12.3 us -> none  [the longest x2 8.19 us: extended_2(): before = lax.ppermute(last, axis, up)]
  transfers between devices with their start and end apart: 5 -> 0, of which waited for: 2 -> 0; matrix products, arithmetic and copies ran while one was open for 2% -> 0% of each run, Pallas kernels for 0% -> 0%
where the time goes in v1:
time: 48.2 us; the launch traced here: 47.8 us
  Pallas kernels  37.1 us (77%)
  local copies, waits for them, and re-layouts  10 us (21%)
  between operations  0.65 us (1%)
    pallas_call x1, Pallas kernels, body(): pl.pallas_call(kernel, out_shape=(jax.ShapeDtypeStruct(velocity.shape, F3...  37.1 us
    unnamed x19, local copies, waits for them, and re-layouts  10 us

profile of v1, /device:TPU:1, one launch (start us, length us, event | category | flops | bytes accessed | tf_op | source)
XLA Modules:
  0.0 47.8 jit_solution(13151428312627494961)
XLA Ops:
  0.6 0.7 %copy.12.owner = s32[64,1]{1,0:T(8,128)S(1)} copy(s32[64,1]{0,1:T(1,128)} %param.14) | data formatting | bytes 512 | tf_op args[6]
  1.4 0.0 copy-start
  1.4 1.4 %copy-done = f32[3,128,1024]{2,1,0:T(8,128)S(1)} copy-done((f32[3,128,1024]{2,1,0:T(8,128)S(1)}, f32[3,128,1024]{2,1,0:T(8,128)}, u32[]{:S(2)}) %copy-start) | copy-done | bytes 1572888
  2.8 0.0 copy-start.1
  2.8 1.2 %copy-done.1 = bf16[1024,512]{1,0:T(8,128)(2,1)S(1)} copy-done((bf16[1024,512]{1,0:T(8,128)(2,1)S(1)}, bf16[1024,512]{1,0:T(8,128)(2,1)}, u32[]{:S(2)}) %copy-start.1) | copy-done | bytes 1048600
  4.0 0.0 copy-start.2
  4.0 1.0 %copy-done.2 = s32[128,1024]{1,0:T(8,128)S(1)} copy-done((s32[128,1024]{1,0:T(8,128)S(1)}, s32[128,1024]{1,0:T(8,128)}, u32[]{:S(2)}) %copy-start.2) | copy-done | bytes 524312
  5.1 0.0 copy-start.3
  5.1 0.9 %copy-done.3 = f32[3,4,8,256]{3,2,1,0:T(8,128)S(1)} copy-done((f32[3,4,8,256]{3,2,1,0:T(8,128)S(1)}, f32[3,4,8,256]{3,2,1,0:T(8,128)}, u32[]{:S(2)}) %copy-start.3) | copy-done | bytes 98328
  5.9 0.0 copy-start.4
  5.9 0.8 %copy-done.4 = f32[4,8,256]{2,1,0:T(8,128)S(1)} copy-done((f32[4,8,256]{2,1,0:T(8,128)S(1)}, f32[4,8,256]{2,1,0:T(8,128)}, u32[]{:S(2)}) %copy-start.4) | copy-done | bytes 32792
  6.7 0.0 copy-start.5
  6.7 0.8 %copy-done.5 = f32[4,8,256]{2,1,0:T(8,128)S(1)} copy-done((f32[4,8,256]{2,1,0:T(8,128)S(1)}, f32[4,8,256]{2,1,0:T(8,128)}, u32[]{:S(2)}) %copy-start.5) | copy-done | bytes 32792
  7.5 0.0 copy-start.6
  7.5 0.8 %copy-done.6 = f32[4,8,256]{2,1,0:T(8,128)S(1)} copy-done((f32[4,8,256]{2,1,0:T(8,128)S(1)}, f32[4,8,256]{2,1,0:T(8,128)}, u32[]{:S(2)}) %copy-start.6) | copy-done | bytes 32792
  8.2 37.1 %shard_map.111 = (f32[3,4,8,256]{3,2,1,0:T(8,128)S(1)}, f32[4,8,256]{2,1,0:T(8,128)S(1)}, f32[4,8,256]{2,1,0:T(8,128)S(1)}, f32[1,768]{1,0:T(1,128)S(1)}) custom-call(f32[3,4,8,256]{3,2,1,0:T(8,128)S(1)} %copy-done.3, f32[4,8,256]{2,1,0:T(8,128)S(1)} %copy-done.4, f32[4,8,256]{2,1,0:T(8,128)S(1)} %copy-done.5, f32[4,8,256]{2,1,0:T(8,128)S(1)} %copy-done.6, ...), custom_call_target="tpu_custom_call" | custom-call | tf_op jit(solution)/shard_map/pallas_call | solution.py:460
  45.3 0.6 %copy.17 = f32[3,4,8,256]{3,2,1,0:T(8,128)} copy(f32[3,4,8,256]{3,2,1,0:T(8,128)S(1)} %get-tuple-element.8) | data formatting | bytes 196608
  45.9 0.6 %copy.18 = f32[4,8,256]{2,1,0:T(8,128)} copy(f32[4,8,256]{2,1,0:T(8,128)S(1)} %get-tuple-element.9) | data formatting | bytes 65536
  46.6 0.6 %copy.19 = f32[4,8,256]{2,1,0:T(8,128)} copy(f32[4,8,256]{2,1,0:T(8,128)S(1)} %get-tuple-element.10) | data formatting | bytes 65536
  47.2 0.6 %copy.20 = f32[1,768]{1,0:T(1,128)} copy(f32[1,768]{1,0:T(1,128)S(1)} %get-tuple-element.11) | data formatting | bytes 6144
Async XLA Ops:
  1.4 1.4 %copy-start = (f32[3,128,1024]{2,1,0:T(8,128)S(1)}, f32[3,128,1024]{2,1,0:T(8,128)}, u32[]{:S(2)}) copy-start(f32[3,128,1024]{2,1,0:T(8,128)} %frac.1) | copy-start | bytes 4718596
  2.8 1.2 %copy-start.1 = (bf16[1024,512]{1,0:T(8,128)(2,1)S(1)}, bf16[1024,512]{1,0:T(8,128)(2,1)}, u32[]{:S(2)}) copy-start(bf16[1024,512]{1,0:T(8,128)(2,1)} %constant.2.clone.ftab) | copy-start | bytes 3145732
  4.0 1.0 %copy-start.2 = (s32[128,1024]{1,0:T(8,128)S(1)}, s32[128,1024]{1,0:T(8,128)}, u32[]{:S(2)}) copy-start(s32[128,1024]{1,0:T(8,128)} %ids.1) | copy-start | bytes 1572868
  5.1 0.9 %copy-start.3 = (f32[3,4,8,256]{3,2,1,0:T(8,128)S(1)}, f32[3,4,8,256]{3,2,1,0:T(8,128)}, u32[]{:S(2)}) copy-start(f32[3,4,8,256]{3,2,1,0:T(8,128)} %vel.1) | copy-start | bytes 294916
  5.9 0.8 %copy-start.4 = (f32[4,8,256]{2,1,0:T(8,128)S(1)}, f32[4,8,256]{2,1,0:T(8,128)}, u32[]{:S(2)}) copy-start(f32[4,8,256]{2,1,0:T(8,128)} %pre.1) | copy-start | bytes 98308
  6.7 0.8 %copy-start.5 = (f32[4,8,256]{2,1,0:T(8,128)S(1)}, f32[4,8,256]{2,1,0:T(8,128)}, u32[]{:S(2)}) copy-start(f32[4,8,256]{2,1,0:T(8,128)} %kin.1) | copy-start | bytes 98308
  7.5 0.8 %copy-start.6 = (f32[4,8,256]{2,1,0:T(8,128)S(1)}, f32[4,8,256]{2,1,0:T(8,128)}, u32[]{:S(2)}) copy-start(f32[4,8,256]{2,1,0:T(8,128)} %dis.1) | copy-start | bytes 98308

commit v2 on v1

v2 whole, which is shorter than its diff:
```python
import functools
import math

import jax
import jax.numpy as jnp
import numpy as np
from jax import lax
from jax.experimental import pallas as pl
from jax.experimental.pallas import tpu as pltpu
from jax.sharding import PartitionSpec as P

F32 = jnp.float32
BF16 = jnp.bfloat16
MESH = pl.DeviceIdType.MESH

base_viscosity = 0.05
time_step = 0.2
beta_star = 0.09
beta_rate = 0.075
alpha_rate = 0.52
wall_rate = 1.0

STREAM = 8
GIRTH = 16
RING = 4
PLANE = 32
CELLS_S = 4
CELLS_G = 8
CELLS_R = 256
AZIMUTHS = 1024
MODES = 128
SECTORS = 64
WIDTH = 16
ROWS = 3 * CELLS_S * CELLS_G
TILES = 24
HALF = TILES // 2
VMEM_BYTES = 64 * 1024 * 1024


def fourier_parts():
    a = np.arange(AZIMUTHS)[:, None]
    h = np.arange(MODES)[None, :]
    angle = (a * h % AZIMUTHS) * (2.0 * math.pi / AZIMUTHS)
    table = np.concatenate([np.cos(angle), -np.sin(angle)], axis=1) / math.sqrt(AZIMUTHS)
    table = table.astype(np.float32)
    high = table.astype(jnp.bfloat16)
    low = (table - high.astype(np.float32)).astype(jnp.bfloat16)
    return np.concatenate([high, low], axis=1)


def parts_of(x, count):
    parts = []
    for _ in range(count):
        part = x.astype(BF16)
        parts.append(part)
        x = x - part.astype(F32)
    return parts


def slope(up1, down1, up2, down2):
    return (8.0 * (up1 - down1) - (up2 - down2)) * (1.0 / 12.0)


def viscosity_of(energy, rate):
    return base_viscosity + energy / (rate + wall_rate)


def lane_shift(x, amount, fill):
    lane = lax.broadcasted_iota(jnp.int32, x.shape, 1)
    rolled = pltpu.roll(x, (-amount) % CELLS_R, axis=1)
    inside = (lane + amount >= 0) & (lane + amount < CELLS_R)
    return jnp.where(inside, rolled, fill)


def flux(center, up, down, v, v_up, v_down):
    return 0.5 * (v + v_up) * (up - center) - 0.5 * (v + v_down) * (center - down)


class Layer:
    def __init__(self, cells, above, wide, s):
        self.cells, self.above, self.wide, self.s = cells, above, wide, s
        self.v = viscosity_of(self.at(4, 0, 0), self.at(5, 0, 0))
        self.v_side = [
            [viscosity_of(self.at(4, d, 0), self.at(5, d, 0)) for d in (1, -1)],
            [viscosity_of(self.at(4, 0, d), self.at(5, 0, d)) for d in (1, -1)],
            [lane_shift(self.v, d, base_viscosity) for d in (1, -1)],
        ]
        self.centers = [self.at(f, 0, 0) for f in range(6)]

    def at(self, f, ds, dg):
        s = self.s
        if dg != 0:
            return self.wide[f, s, 8 + dg : 16 + dg, :]
        if s + ds < 0:
            return self.above[0, f, 2 + s + ds]
        if s + ds >= CELLS_S:
            return self.above[1, f, s + ds - CELLS_S]
        return self.cells[f, s + ds]

    def around(self, f, d):
        if d == 0:
            return [self.at(f, j, 0) for j in (1, -1, 2, -2)]
        if d == 1:
            return [self.at(f, 0, j) for j in (1, -1, 2, -2)]
        return [lane_shift(self.centers[f], j, 0.0) for j in (1, -1, 2, -2)]

    def diffuse(self, f, near, d):
        return flux(self.centers[f], near[0], near[1], self.v, *self.v_side[d])

    def velocity(self):
        strain = None
        updated = []
        for c in range(3):
            change = -slope(*self.around(3, c))
            for d in range(3):
                near = self.around(c, d)
                gradient = slope(*near)
                square = gradient * gradient
                strain = square if strain is None else strain + square
                change = change - self.centers[d] * gradient
                change = change + self.diffuse(c, near, d)
            updated.append(self.centers[c] + time_step * change)
        return updated, strain

    def turbulence(self, strain):
        k, w = self.centers[4], self.centers[5]
        changes = [
            k / (w + wall_rate) * strain - beta_star * k * w,
            alpha_rate * strain - beta_rate * w * w,
        ]
        updated = []
        for change, f in zip(changes, (4, 5)):
            for d in range(3):
                near = self.around(f, d)
                change = change - self.centers[d] * slope(*near)
                change = change + self.diffuse(f, near, d)
            updated.append(self.centers[f] + time_step * change)
        return updated


def point_tiles(a):
    lane = lax.broadcasted_iota(jnp.int32, (16, 128), 1)
    first = jnp.concatenate([a[0:16, 0:128], a[16:32, 0:128]], axis=1)
    rest = jnp.where(lane < 64, a[0:16, 128:256], a[16:32, 128:256])
    tiles = []
    for h in range(2):
        tiles.append(first[8 * h : 8 * h + 8])
        both = [rest[8 * h : 8 * h + 4], rest[8 * h + 4 : 8 * h + 8]]
        tiles.append(jnp.concatenate(both, axis=1))
    return jnp.concatenate(tiles, axis=0)


def radius_rows(d):
    lane = lax.broadcasted_iota(jnp.int32, (8, 128), 1)
    rest = jnp.concatenate([d[8:12, 0:128], d[8:12, 128:256]], axis=0)
    low = jnp.where(lane < 64, rest, 0.0)
    high = jnp.where(lane < 64, 0.0, rest)
    return jnp.concatenate(
        [
            jnp.concatenate([d[0:8, 0:128], low], axis=1),
            jnp.concatenate([d[0:8, 128:256], high], axis=1),
        ],
        axis=0,
    )


def kernel(
    vel, pre, kin, dis, ids, frac, owner, ftab,
    nv_o, ne_o, nr_o, harm_o,
    cells, above, wide, pack, edge, nv, strain_v, turb, ids_v, frac_v, ft, choose, W, lhs, vec,
    acc, disk, four, sendb, recvb,
    in_sem, out_sem, hs_sem, hr_sem, gs_sem, gr_sem, as_sem, ar_sem,
):
    t = lax.axis_index("stream")
    g = lax.axis_index("girth")
    y = t // RING
    z = lax.rem(t, RING)
    me = y * GIRTH + g

    own = [
        pltpu.make_async_copy(vel, cells.at[0:3], in_sem.at[0]),
        pltpu.make_async_copy(pre, cells.at[3], in_sem.at[1]),
        pltpu.make_async_copy(kin, cells.at[4], in_sem.at[2]),
        pltpu.make_async_copy(dis, cells.at[5], in_sem.at[3]),
    ]
    for copy in own:
        copy.start()

    barrier = pltpu.get_barrier_semaphore()

    def plane_peer(i):
        other = lax.rem(me + i, PLANE)
        return other, (other // GIRTH * RING + z, lax.rem(other, GIRTH))

    def ring_peer(i):
        return (y * RING + lax.rem(z + i, RING), g)

    def greet(i, carry):
        pl.semaphore_signal(barrier, inc=1, device_id=plane_peer(i)[1], device_id_type=MESH)
        return carry

    seam_up = t == RING - 1
    seam_down = t == RING

    @pl.when(seam_up)
    def _():
        pl.semaphore_signal(barrier, inc=1, device_id=(t + 1, g), device_id_type=MESH)

    @pl.when(seam_down)
    def _():
        pl.semaphore_signal(barrier, inc=1, device_id=(t - 1, g), device_id_type=MESH)

    for i in (1, RING - 1, 2):
        pl.semaphore_signal(barrier, inc=1, device_id=ring_peer(i), device_id_type=MESH)
    greet(1, 0)
    greet(PLANE - 1, 0)
    lax.fori_loop(2, PLANE - 1, greet, 0)

    points = []
    for half in range(2):
        rows = pl.ds((half * RING + z) * GIRTH, GIRTH)
        points.append(
            pltpu.make_async_copy(ids.at[rows, :], ids_v.at[half], in_sem.at[4 + half])
        )
        points.append(
            pltpu.make_async_copy(frac.at[:, rows, :], frac_v.at[half], in_sem.at[6 + half])
        )
    points.append(pltpu.make_async_copy(ftab, ft, in_sem.at[8]))

    seam = jnp.where(seam_up | seam_down, 1, 0)
    pl.semaphore_wait(barrier, PLANE - 1 + RING - 1 + seam)

    def halo(k):
        if k < 8:
            down = k < 4
            field, place = ((vel, pl.ds(0, 3)), (pre, 3), (kin, 4), (dis, 5))[k % 4]
            layers_of = pl.ds(0, 2) if down else pl.ds(2, 2)
            src = field.at[:, layers_of] if k % 4 == 0 else field.at[layers_of]
            dst = above.at[1 if down else 0, place]
            dev = (t - 1, g) if down else (t + 1, g)
        elif k == 8:
            src, dst, dev = pack.at[0], edge.at[1], (t, g - 1)
        else:
            src, dst, dev = pack.at[1], edge.at[0], (t, g + 1)
        return pltpu.make_async_remote_copy(
            src_ref=src, dst_ref=dst, send_sem=hs_sem.at[k], recv_sem=hr_sem.at[k],
            device_id=dev, device_id_type=MESH,
        )

    sides = (range(0, 4), range(4, 8), range(8, 9), range(9, 10))
    sends = (t > 0, t < STREAM - 1, g > 0, g < GIRTH - 1)
    receives = (sends[1], sends[0], sends[3], sends[2])

    def each(side, there, act):
        @pl.when(there[side])
        def _():
            for k in sides[side]:
                act(halo(k))

    for side in (0, 1):
        each(side, sends, lambda copy: copy.start())
    for copy in own:
        copy.wait()
    for f in range(6):
        for s in range(CELLS_S):
            pack[0, f, 2 * s : 2 * s + 2, :] = cells[f, s, 0:2, :]
            pack[1, f, 2 * s : 2 * s + 2, :] = cells[f, s, 6:8, :]
    for side in (2, 3):
        each(side, sends, lambda copy: copy.start())
    for copy in points:
        copy.start()
    for f in range(6):
        for s in range(CELLS_S):
            wide[f, s, 8:16, :] = cells[f, s]

    @pl.when(t == 0)
    def _():
        above[0] = jnp.zeros((6, 2, 8, CELLS_R), F32)

    @pl.when(t == STREAM - 1)
    def _():
        above[1] = jnp.zeros((6, 2, 8, CELLS_R), F32)

    @pl.when(g == 0)
    def _():
        edge[0] = jnp.zeros((6, 8, CELLS_R), F32)

    @pl.when(g == GIRTH - 1)
    def _():
        edge[1] = jnp.zeros((6, 8, CELLS_R), F32)

    sub8 = lax.broadcasted_iota(jnp.int32, (8, 128), 0)
    lane8 = lax.broadcasted_iota(jnp.int32, (8, 128), 1)

    def sector(s, carry):
        count, place = carry
        mine = jnp.where(owner[s] == g, 1, 0)
        here = (sub8 == s // 8) & (lane8 // WIDTH == lax.rem(s, 8))
        value = jnp.where(mine > 0, count * WIDTH, -AZIMUTHS) + lax.rem(lane8, WIDTH)
        return count + mine, jnp.where(here, value, place)

    _, place = lax.fori_loop(
        0, SECTORS, sector, (jnp.int32(0), jnp.full((8, 128), -AZIMUTHS, jnp.int32))
    )
    row = lax.broadcasted_iota(jnp.int32, (256, 128), 0)
    slot = jnp.where(row < 192, row, row - 64)
    for k in range(8):
        hit = slot == place[k : k + 1, :]
        choose[:, k * 128 : (k + 1) * 128] = jnp.where(hit, 1.0, 0.0).astype(BF16)

    for copy in points:
        copy.wait()
    cid = ids_v[...].reshape(PLANE, AZIMUTHS)
    stream_cell = lax.shift_right_logical(cid, 11)
    girth_cell = lax.shift_right_logical(cid, 8) & 7
    wall_cell = cid & 255
    stack = [wall_cell.astype(F32).astype(BF16), stream_cell.astype(F32).astype(BF16)]
    stack.append(girth_cell.astype(F32).astype(BF16))
    for i in range(3):
        stack.extend(parts_of(frac_v[:, i].reshape(PLANE, AZIMUTHS), 3))
    picked = lax.dot_general(
        jnp.concatenate(stack, axis=0), choose[...], (((1,), (1,)), ((), ())),
        preferred_element_type=F32,
    )
    part = [picked[32 * i : 32 * i + 32] for i in range(12)]
    cell_q, cell_s, cell_g = [point_tiles(part[i]) for i in range(3)]
    f_s, f_g, f_q = [
        point_tiles(part[3 + 3 * i] + part[4 + 3 * i] + part[5 + 3 * i]) for i in range(3)
    ]
    vec[0] = cell_s
    vec[1] = f_s
    vec[2] = cell_g
    vec[3] = f_g
    vec[4] = cell_q
    low_parts = parts_of(1.0 - f_q, 2)
    high_parts = parts_of(f_q, 2)
    vec[5] = low_parts[0].astype(F32)
    vec[6] = low_parts[1].astype(F32)
    vec[7] = high_parts[0].astype(F32)
    vec[8] = high_parts[1].astype(F32)

    chosen = jnp.dot(choose[...], ft[...], preferred_element_type=F32).astype(BF16)
    four[0:256, :] = chosen[:, 0:256]
    four[256:512, :] = chosen[:, 256:512]

    def weights(n, carry):
        def v(i):
            return vec[i, pl.ds(n, 1), :]

        q = lax.broadcasted_iota(jnp.int32, (CELLS_R, 256), 0).astype(F32)
        at_q = q == v(4)
        at_up = q == v(4) + 1.0
        high = jnp.where(at_q, v(5), jnp.where(at_up, v(7), 0.0)).astype(BF16)
        low = jnp.where(at_q, v(6), jnp.where(at_up, v(8), 0.0)).astype(BF16)
        cols = pl.ds(pl.multiple_of(n * 256, 256), 256)
        W[0:256, cols] = high
        W[256:512, cols] = low
        return carry

    lax.fori_loop(0, TILES, weights, 0, unroll=2)
    sendb[...] = jnp.zeros_like(sendb)

    for side in range(4):
        each(side, receives, lambda copy: copy.wait_recv())
    for f in range(6):
        for s in range(CELLS_S):
            wide[f, s, 6:8, :] = edge[0, f, 2 * s : 2 * s + 2, :]
            wide[f, s, 16:18, :] = edge[1, f, 2 * s : 2 * s + 2, :]

    def gather(i, s):
        return pltpu.make_async_remote_copy(
            src_ref=nv.at[0, s], dst_ref=nv.at[RING - i, s],
            send_sem=gs_sem.at[i * CELLS_S + s], recv_sem=gr_sem.at[i * CELLS_S + s],
            device_id=ring_peer(i), device_id_type=MESH,
        )

    for s in range(CELLS_S):
        updated, strain = Layer(cells, above, wide, s).velocity()
        for c in range(3):
            nv[0, s, c] = updated[c]
        strain_v[s] = strain
        for i in (2, 1, 3):
            gather(i, s).start()
    for s in range(CELLS_S):
        turb[0, s], turb[1, s] = Layer(cells, above, wide, s).turbulence(strain_v[s])
    results = [
        pltpu.make_async_copy(nv.at[0, s], nv_o.at[:, s], out_sem.at[s]) for s in range(CELLS_S)
    ]
    results.append(pltpu.make_async_copy(turb.at[0], ne_o, out_sem.at[4]))
    results.append(pltpu.make_async_copy(turb.at[1], nr_o, out_sem.at[5]))
    for copy in results:
        copy.start()

    def load_blocks(first, count):
        value = jnp.concatenate(
            [nv[first + b].reshape(ROWS, CELLS_R) for b in range(count)], axis=0
        )
        high, low = parts_of(value, 2)
        start = 2 * first * ROWS
        lhs[start : start + count * ROWS, :] = high
        lhs[start + count * ROWS : start + 2 * count * ROWS, :] = low

    def layers(blocks, n, sums):
        first, count = blocks
        start, rows = 2 * first * ROWS, count * ROWS
        cols = pl.ds(pl.multiple_of(n * 256, 256), 256)
        both = jnp.dot(
            lhs[start : start + 2 * rows, :], W[0:256, cols], preferred_element_type=F32
        )
        fine = jnp.dot(lhs[start : start + rows, :], W[256:512, cols], preferred_element_type=F32)
        out = both[0:rows] + both[rows : 2 * rows] + fine
        cell = jnp.broadcast_to(vec[0, pl.ds(n, 1), :], (8, 256))
        up = jnp.broadcast_to(vec[1, pl.ds(n, 1), :], (8, 256))
        stay = 1.0 - up
        for b in range(count):
            base = ((y * RING + lax.rem(z + first + b, RING)) * CELLS_S).astype(F32)
            above_base = cell - base
            for s in range(CELLS_S):
                weight = jnp.where(
                    above_base == s, stay, jnp.where(above_base == s - 1, up, 0.0)
                )
                for c in range(3):
                    at = b * ROWS + s * 24 + c * 8
                    term = weight * out[at : at + 8]
                    sums[c] = term if sums[c] is None else sums[c] + term
        return sums

    load_blocks(0, 1)

    def first_pass(n, carry):
        sums = layers((0, 1), n, [None] * 3)
        for c in range(3):
            acc[c * TILES + n] = sums[c]
        return carry

    lax.fori_loop(0, TILES, first_pass, 0, unroll=4)

    for i in range(1, RING):
        for s in range(CELLS_S):
            gather(i, s).wait_recv()
    load_blocks(1, RING - 1)

    near = g // 8
    my_slot = y * 8 + lax.rem(g, 8)

    def slot_of(i):
        return pl.ds(pl.multiple_of(i * 8, 8), 8)

    def post(turn, j):
        half = 1 - near if turn == 0 else near
        slot = lax.rem(my_slot + j, 16)
        dev = (slot // 8 * RING + z, half * 8 + lax.rem(slot, 8))
        return pltpu.make_async_remote_copy(
            src_ref=sendb.at[slot_of(16 * turn + slot), :],
            dst_ref=recvb.at[slot_of(16 * turn + j), :],
            send_sem=as_sem.at[turn], recv_sem=ar_sem.at[turn],
            device_id=dev, device_id_type=MESH,
        )

    def posts(turn):
        span = pl.ds(128 * turn + 8 * turn, 128 - 8 * turn)
        return pltpu.make_async_remote_copy(
            src_ref=sendb.at[span, :], dst_ref=recvb.at[span, :],
            send_sem=as_sem.at[turn], recv_sem=ar_sem.at[turn],
            device_id=plane_peer(1)[1], device_id_type=MESH,
        )

    for turn in range(2):
        offset = ((1 - near) if turn == 0 else near) * HALF

        def second_pass(k, carry, offset=offset):
            n = offset + k
            sums = layers((1, 3), n, [acc[c * TILES + n] for c in range(3)])
            cell = vec[2, pl.ds(n, 1), :]
            up = vec[3, pl.ds(n, 1), :]
            side = lax.broadcasted_iota(jnp.int32, (8, 256), 0).astype(F32)
            weight = jnp.where(side == cell, 1.0 - up, jnp.where(side == cell + 1.0, up, 0.0))
            for c in range(3):
                disk[pl.ds(c * 16 + k, 1), :] = jnp.sum(sums[c] * weight, axis=0, keepdims=True)
            return carry

        lax.fori_loop(0, HALF, second_pass, 0, unroll=4)
        rows = jnp.concatenate(
            [radius_rows(disk[c * 16 : c * 16 + HALF, :]) for c in range(3)], axis=0
        )
        high, low = parts_of(rows, 2)
        both = jnp.dot(
            jnp.concatenate([high, low], axis=0), four[0:256, :], preferred_element_type=F32
        )
        fine = jnp.dot(high, four[256:512, :], preferred_element_type=F32)
        spectrum = both[0:48] + both[48:96] + fine
        for c in range(3):
            for k in range(2):
                sendb[pl.ds(128 * turn + 2 * c + k, 16, stride=8), :] = spectrum[
                    c * 16 : (c + 1) * 16, k * 128 : (k + 1) * 128
                ]

        def post_one(j, carry, turn=turn):
            post(turn, j).start()
            return carry

        lax.fori_loop(turn, 16, post_one, 0)

    total = sendb[slot_of(16 + my_slot), :]
    for turn in range(2):
        posts(turn).wait_recv()
        for j in range(turn, 16):
            row = 128 * turn + 8 * j
            total = total + recvb[row : row + 8, :]
    for k in range(6):
        harm_o[0:1, k * 128 : (k + 1) * 128] = total[k : k + 1, :]

    for side in range(4):
        each(side, sends, lambda copy: copy.wait_send())
    for i in range(1, RING):
        for s in range(CELLS_S):
            gather(i, s).wait_send()
    for copy in results:
        copy.wait()
    for turn in range(2):
        posts(turn).wait_send()


def place_results(*refs):
    count = len(refs) // 2
    for i in range(count):
        refs[count + i][...] = refs[i][...]


def body(velocity, pressure, kinetic_energy, dissipation_rate, corner_ids, fractions, sector_owner):
    hbm = pl.BlockSpec(memory_space=pltpu.HBM)
    vmem = pl.BlockSpec(memory_space=pltpu.VMEM)
    smem = pl.BlockSpec(memory_space=pltpu.SMEM)
    dma = pltpu.SemaphoreType.DMA
    shapes = (
        jax.ShapeDtypeStruct(velocity.shape, F32),
        jax.ShapeDtypeStruct(pressure.shape, F32),
        jax.ShapeDtypeStruct(pressure.shape, F32),
        jax.ShapeDtypeStruct((1, 6 * MODES), F32),
    )
    results = pl.pallas_call(
        kernel,
        out_shape=shapes,
        in_specs=[hbm] * 6 + [smem, hbm],
        out_specs=(hbm, hbm, hbm, vmem),
        scratch_shapes=[
            pltpu.VMEM((6, CELLS_S, CELLS_G, CELLS_R), F32),
            pltpu.VMEM((2, 6, 2, CELLS_G, CELLS_R), F32),
            pltpu.VMEM((6, CELLS_S, 24, CELLS_R), F32),
            pltpu.VMEM((2, 6, 8, CELLS_R), F32),
            pltpu.VMEM((2, 6, 8, CELLS_R), F32),
            pltpu.VMEM((RING, CELLS_S, 3, CELLS_G, CELLS_R), F32),
            pltpu.VMEM((CELLS_S, CELLS_G, CELLS_R), F32),
            pltpu.VMEM((2, CELLS_S, CELLS_G, CELLS_R), F32),
            pltpu.VMEM((2, GIRTH, AZIMUTHS), jnp.int32),
            pltpu.VMEM((2, 3, GIRTH, AZIMUTHS), F32),
            pltpu.VMEM((AZIMUTHS, 512), BF16),
            pltpu.VMEM((256, AZIMUTHS), BF16),
            pltpu.VMEM((512, TILES * 256), BF16),
            pltpu.VMEM((2 * RING * ROWS, 256), BF16),
            pltpu.VMEM((9, TILES, 256), F32),
            pltpu.VMEM((3 * TILES, 8, 256), F32),
            pltpu.VMEM((48, 256), F32),
            pltpu.VMEM((512, 256), BF16),
            pltpu.VMEM((PLANE * 8, 128), F32),
            pltpu.VMEM((PLANE * 8, 128), F32),
            dma((9,)),
            dma((6,)),
            dma((10,)),
            dma((10,)),
            dma((RING * CELLS_S,)),
            dma((RING * CELLS_S,)),
            dma((2,)),
            dma((2,)),
        ],
        compiler_params=pltpu.CompilerParams(
            collective_id=0, has_side_effects=True, vmem_limit_bytes=VMEM_BYTES
        ),
    )(
        velocity, pressure, kinetic_energy, dissipation_rate, corner_ids, fractions,
        sector_owner.reshape(SECTORS), jnp.asarray(fourier_parts()),
    )
    return pl.pallas_call(
        place_results,
        out_shape=shapes,
        in_specs=[vmem] * 4,
        out_specs=(vmem,) * 4,
        compiler_params=pltpu.CompilerParams(vmem_limit_bytes=VMEM_BYTES),
    )(*results)


def solution(mesh):
    return jax.shard_map(
        body,
        mesh=mesh,
        in_specs=(
            P(None, "stream", "girth", None),
            P("stream", "girth", None),
            P("stream", "girth", None),
            P("stream", "girth", None),
            P(),
            P(),
            P(),
        ),
        out_specs=(
            P(None, "stream", "girth", None),
            P("stream", "girth", None),
            P("stream", "girth", None),
            P(("stream", "girth"), None),
        ),
        check_vma=False,
    )
```

time: 48.2 us -> 33.3 us (0.69)
  local copies, waits for them, and re-layouts: 10 us -> 0 us
  Pallas kernels: 37.1 us -> 32.4 us
    unnamed x19 -> x0, local copies, waits for them, and re-layouts: 10 us -> none
    pallas_call x1 -> x2, Pallas kernels: 37.1 us -> 32.4 us  [the longest x1 30.8 us: body(): pl.pallas_call(kernel, out_shape=shapes, in_specs=[hbm] * 6 + [smem, hbm]...]
where the time goes in v2:
time: 33.3 us; the launch traced here: 33.1 us
  Pallas kernels  32.4 us (97%)
  between operations  0.64 us (2%)
    pallas_call x1, Pallas kernels, body(): pl.pallas_call(kernel, out_shape=shapes, in_specs=[hbm] * 6 + [smem, hbm]...  30.8 us
    pallas_call x1, Pallas kernels, body(): pl.pallas_call(place_results, out_shape=shapes, in_specs=[vmem] * 4, out_...  1.58 us

profile of v2, /device:TPU:1, one launch (start us, length us, event | category | flops | bytes accessed | tf_op | source)
XLA Modules:
  0.0 33.1 jit_solution(5927182240702570120)
XLA Ops:
  0.6 30.8 %shard_map.111 = (f32[3,4,8,256]{3,2,1,0:T(8,128)}, f32[4,8,256]{2,1,0:T(8,128)}, f32[4,8,256]{2,1,0:T(8,128)}, f32[1,768]{1,0:T(1,128)}) custom-call(f32[3,4,8,256]{3,2,1,0:T(8,128)} %vel.1, f32[4,8,256]{2,1,0:T(8,128)} %pre.1, f32[4,8,256]{2,1,0:T(8,128)} %kin.1, f32[4,8,256]{2,1,0:T(8,128)} %dis.1, s32[128,1024]{1,0:T(8,128)} %ids.1, ...), custom_call_target="tpu_custom_call" | custom-call | tf_op jit(solution)/shard_map/pallas_call | solution.py:541
  31.5 1.6 %shard_map.112 = (f32[3,4,8,256]{3,2,1,0:T(8,128)}, f32[4,8,256]{2,1,0:T(8,128)}, f32[4,8,256]{2,1,0:T(8,128)}, f32[1,768]{1,0:T(1,128)}) custom-call(f32[3,4,8,256]{3,2,1,0:T(8,128)} %get-tuple-element.8.refs_0_, f32[4,8,256]{2,1,0:T(8,128)} %get-tuple-element.9.refs_1_, f32[4,8,256]{2,1,0:T(8,128)} %get-tuple-element.10.refs_2_, ...), custom_call_target="tpu_custom_call" | custom-call | tf_op jit(solution)/shard_map/pallas_call | solution.py:583

commit v3 on v2

--- a/solution.py
+++ b/solution.py
@@ -166,16 +166,16 @@
 
 def kernel(
     vel, pre, kin, dis, ids, frac, owner, ftab,
-    nv_o, ne_o, nr_o, harm_o,
+    nv_o, ne_o, nr_o, recvb,
     cells, above, wide, pack, edge, nv, strain_v, turb, ids_v, frac_v, ft, choose, W, lhs, vec,
-    acc, disk, four, sendb, recvb,
-    in_sem, out_sem, hs_sem, hr_sem, gs_sem, gr_sem, as_sem, ar_sem,
+    acc, disk, four, sendb,
+    in_sem, out_sem, hs_sem, hr_sem, gs_sem, gr_sem, as_sem, ar_sem, row_sem, plane_sem,
 ):
     t = lax.axis_index("stream")
     g = lax.axis_index("girth")
     y = t // RING
     z = lax.rem(t, RING)
-    me = y * GIRTH + g
+    other_t = jnp.where(t < RING, t + RING, t - RING)
 
     own = [
         pltpu.make_async_copy(vel, cells.at[0:3], in_sem.at[0]),
@@ -188,33 +188,50 @@
 
     barrier = pltpu.get_barrier_semaphore()
 
-    def plane_peer(i):
-        other = lax.rem(me + i, PLANE)
-        return other, (other // GIRTH * RING + z, lax.rem(other, GIRTH))
+    def plane_peer(across, step):
+        turned = g + step
+        turned = jnp.where(turned >= GIRTH, turned - GIRTH, turned)
+        return (other_t if across else t, turned)
 
     def ring_peer(i):
         return (y * RING + lax.rem(z + i, RING), g)
 
-    def greet(i, carry):
-        pl.semaphore_signal(barrier, inc=1, device_id=plane_peer(i)[1], device_id_type=MESH)
-        return carry
+    def greet(device):
+        pl.semaphore_signal(barrier, inc=1, device_id=device, device_id_type=MESH)
 
     seam_up = t == RING - 1
     seam_down = t == RING
 
     @pl.when(seam_up)
     def _():
-        pl.semaphore_signal(barrier, inc=1, device_id=(t + 1, g), device_id_type=MESH)
+        greet((t + 1, g))
 
     @pl.when(seam_down)
     def _():
-        pl.semaphore_signal(barrier, inc=1, device_id=(t - 1, g), device_id_type=MESH)
-
-    for i in (1, RING - 1, 2):
-        pl.semaphore_signal(barrier, inc=1, device_id=ring_peer(i), device_id_type=MESH)
-    greet(1, 0)
-    greet(PLANE - 1, 0)
-    lax.fori_loop(2, PLANE - 1, greet, 0)
+        greet((t - 1, g))
+
+    core = lax.rem(g, 4)
+    edge_up = (core == 3) & (g < GIRTH - 1)
+    edge_down = (core == 0) & (g > 0)
+
+    @pl.when(edge_up)
+    def _():
+        greet((t, g + 1))
+
+    @pl.when(edge_down)
+    def _():
+        greet((t, g - 1))
+
+    for i in (1, RING - 1):
+        greet(ring_peer(i))
+    same_x = []
+    for step in range(1, 4):
+        turned = core + step
+        same_x.append((t, g - core + jnp.where(turned >= 4, turned - 4, turned)))
+    other_x = [plane_peer(False, 4 * step) for step in range(1, 4)]
+    across = plane_peer(True, 0)
+    for device in same_x + other_x + [across]:
+        greet(device)
 
     points = []
     for half in range(2):
@@ -227,8 +244,8 @@
         )
     points.append(pltpu.make_async_copy(ftab, ft, in_sem.at[8]))
 
-    seam = jnp.where(seam_up | seam_down, 1, 0)
-    pl.semaphore_wait(barrier, PLANE - 1 + RING - 1 + seam)
+    seam = jnp.where(seam_up | seam_down, 1, 0) + jnp.where(edge_up | edge_down, 1, 0)
+    pl.semaphore_wait(barrier, 2 + 3 + 3 + 1 + seam)
 
     def halo(k):
         if k < 8:
@@ -269,6 +286,8 @@
         each(side, sends, lambda copy: copy.start())
     for copy in points:
         copy.start()
+    for device in other_x:
+        pl.semaphore_signal(row_sem, inc=1, device_id=device, device_id_type=MESH)
     for f in range(6):
         for s in range(CELLS_S):
             wide[f, s, 8:16, :] = cells[f, s]
@@ -360,6 +379,9 @@
     lax.fori_loop(0, TILES, weights, 0, unroll=2)
     sendb[...] = jnp.zeros_like(sendb)
 
+    pl.semaphore_wait(row_sem, 3)
+    pl.semaphore_signal(plane_sem, inc=1, device_id=across, device_id_type=MESH)
+
     for side in range(4):
         each(side, receives, lambda copy: copy.wait_recv())
     for f in range(6):
@@ -441,18 +463,20 @@
     load_blocks(1, RING - 1)
 
     near = g // 8
-    my_slot = y * 8 + lax.rem(g, 8)
+    column = lax.rem(g, 8)
 
     def slot_of(i):
         return pl.ds(pl.multiple_of(i * 8, 8), 8)
 
     def post(turn, j):
         half = 1 - near if turn == 0 else near
-        slot = lax.rem(my_slot + j, 16)
-        dev = (slot // 8 * RING + z, half * 8 + lax.rem(slot, 8))
+        turned = column + j % 8
+        turned = jnp.where(turned >= 8, turned - 8, turned)
+        across = 1 - y if j >= 8 else y
+        dev = (other_t if j >= 8 else t, half * 8 + turned)
         return pltpu.make_async_remote_copy(
-            src_ref=sendb.at[slot_of(16 * turn + slot), :],
-            dst_ref=recvb.at[slot_of(16 * turn + j), :],
+            src_ref=sendb.at[slot_of(16 * turn + across * 8 + turned), :],
+            dst_ref=recvb.at[pl.ds(8 * (16 * turn + j), 8), :],
             send_sem=as_sem.at[turn], recv_sem=ar_sem.at[turn],
             device_id=dev, device_id_type=MESH,
         )
@@ -462,9 +486,10 @@
         return pltpu.make_async_remote_copy(
             src_ref=sendb.at[span, :], dst_ref=recvb.at[span, :],
             send_sem=as_sem.at[turn], recv_sem=ar_sem.at[turn],
-            device_id=plane_peer(1)[1], device_id_type=MESH,
-        )
-
+            device_id=plane_peer(True, 0), device_id_type=MESH,
+        )
+
+    pl.semaphore_wait(plane_sem, 1)
     for turn in range(2):
         offset = ((1 - near) if turn == 0 else near) * HALF
 
@@ -479,7 +504,7 @@
                 disk[pl.ds(c * 16 + k, 1), :] = jnp.sum(sums[c] * weight, axis=0, keepdims=True)
             return carry
 
-        lax.fori_loop(0, HALF, second_pass, 0, unroll=4)
+        lax.fori_loop(0, HALF, second_pass, 0, unroll=12)
         rows = jnp.concatenate(
             [radius_rows(disk[c * 16 : c * 16 + HALF, :]) for c in range(3)], axis=0
         )
@@ -495,21 +520,14 @@
                     c * 16 : (c + 1) * 16, k * 128 : (k + 1) * 128
                 ]
 
-        def post_one(j, carry, turn=turn):
+        for j in range(15, turn - 1, -1):
             post(turn, j).start()
-            return carry
-
-        lax.fori_loop(turn, 16, post_one, 0)
-
-    total = sendb[slot_of(16 + my_slot), :]
-    for turn in range(2):
-        posts(turn).wait_recv()
-        for j in range(turn, 16):
-            row = 128 * turn + 8 * j
-            total = total + recvb[row : row + 8, :]
-    for k in range(6):
-        harm_o[0:1, k * 128 : (k + 1) * 128] = total[k : k + 1, :]
-
+
+    mine = pltpu.make_async_copy(
+        sendb.at[slot_of(16 + y * 8 + column), :], recvb.at[pl.ds(128, 8), :], out_sem.at[6]
+    )
+    mine.start()
+    results.append(mine)
     for side in range(4):
         each(side, sends, lambda copy: copy.wait_send())
     for i in range(1, RING):
@@ -519,12 +537,16 @@
         copy.wait()
     for turn in range(2):
         posts(turn).wait_send()
-
-
-def place_results(*refs):
-    count = len(refs) // 2
-    for i in range(count):
-        refs[count + i][...] = refs[i][...]
+        posts(turn).wait_recv()
+
+
+def place_results(nv, ne, nr, parts, nv_o, ne_o, nr_o, harm_o):
+    nv_o[...] = nv[...]
+    ne_o[...] = ne[...]
+    nr_o[...] = nr[...]
+    total = jnp.sum(parts[...].reshape(PLANE, 8, 128), axis=0)
+    for k in range(6):
+        harm_o[0:1, k * 128 : (k + 1) * 128] = total[k : k + 1, :]
 
 
 def body(velocity, pressure, kinetic_energy, dissipation_rate, corner_ids, fractions, sector_owner):
@@ -540,9 +562,9 @@
     )
     results = pl.pallas_call(
         kernel,
-        out_shape=shapes,
+        out_shape=shapes[:3] + (jax.ShapeDtypeStruct((PLANE * 8, 128), F32),),
         in_specs=[hbm] * 6 + [smem, hbm],
-        out_specs=(hbm, hbm, hbm, vmem),
+        out_specs=(hbm,) * 4,
         scratch_shapes=[
             pltpu.VMEM((6, CELLS_S, CELLS_G, CELLS_R), F32),
             pltpu.VMEM((2, 6, 2, CELLS_G, CELLS_R), F32),
@@ -563,15 +585,16 @@
             pltpu.VMEM((48, 256), F32),
             pltpu.VMEM((512, 256), BF16),
             pltpu.VMEM((PLANE * 8, 128), F32),
-            pltpu.VMEM((PLANE * 8, 128), F32),
             dma((9,)),
-            dma((6,)),
+            dma((7,)),
             dma((10,)),
             dma((10,)),
             dma((RING * CELLS_S,)),
             dma((RING * CELLS_S,)),
             dma((2,)),
             dma((2,)),
+            pltpu.SemaphoreType.REGULAR,
+            pltpu.SemaphoreType.REGULAR,
         ],
         compiler_params=pltpu.CompilerParams(
             collective_id=0, has_side_effects=True, vmem_limit_bytes=VMEM_BYTES

time: 33.3 us -> 29.7 us (0.89)
  Pallas kernels: 32.4 us -> 28.9 us
    pallas_call x1, Pallas kernels: 30.8 us -> 27.3 us  [body(): pl.pallas_call(kernel, out_shape=shapes[:3] + (jax.ShapeDtypeStruct((PLAN...]
where the time goes in v3:
time: 29.7 us; the launch traced here: 29.6 us
  Pallas kernels  28.9 us (97%)
  between operations  0.64 us (2%)
    pallas_call x1, Pallas kernels, body(): pl.pallas_call(kernel, out_shape=shapes[:3] + (jax.ShapeDtypeStruct((PLAN...  27.3 us
    pallas_call x1, Pallas kernels, body(): pl.pallas_call(place_results, out_shape=shapes, in_specs=[vmem] * 4, out_...  1.66 us

profile of v3, /device:TPU:1, one launch (start us, length us, event | category | flops | bytes accessed | tf_op | source)
XLA Modules:
  0.0 29.6 jit_solution(13131496292247078042)
XLA Ops:
  0.6 27.3 %shard_map.111 = (f32[3,4,8,256]{3,2,1,0:T(8,128)}, f32[4,8,256]{2,1,0:T(8,128)}, f32[4,8,256]{2,1,0:T(8,128)}, f32[256,128]{1,0:T(8,128)}) custom-call(f32[3,4,8,256]{3,2,1,0:T(8,128)} %vel.1, f32[4,8,256]{2,1,0:T(8,128)} %pre.1, f32[4,8,256]{2,1,0:T(8,128)} %kin.1, f32[4,8,256]{2,1,0:T(8,128)} %dis.1, s32[128,1024]{1,0:T(8,128)} %ids.1, ...), custom_call_target="tpu_custom_call" | custom-call | tf_op jit(solution)/shard_map/pallas_call | solution.py:563
  27.9 1.7 %shard_map.112 = (f32[3,4,8,256]{3,2,1,0:T(8,128)}, f32[4,8,256]{2,1,0:T(8,128)}, f32[4,8,256]{2,1,0:T(8,128)}, f32[1,768]{1,0:T(1,128)}) custom-call(f32[3,4,8,256]{3,2,1,0:T(8,128)} %get-tuple-element.8.nv, f32[4,8,256]{2,1,0:T(8,128)} %get-tuple-element.9.ne, f32[4,8,256]{2,1,0:T(8,128)} %get-tuple-element.10.nr, f32[256,128]{1,0:T(8,128)} %get-tuple-element.11.parts), custom_call_target="tpu_custom_call" | custom-call | tf_op jit(solution)/shard_map/pallas_call | solution.py:606

commit v4 on v3

--- a/solution.py
+++ b/solution.py
@@ -165,9 +165,9 @@
 
 
 def kernel(
-    vel, pre, kin, dis, ids, frac, owner, ftab,
+    vel, pre, kin, dis, ids, frac, owner_in, ftab,
     nv_o, ne_o, nr_o, recvb,
-    cells, above, wide, pack, edge, nv, strain_v, turb, ids_v, frac_v, ft, choose, W, lhs, vec,
+    owner, cells, above, wide, pack, edge, nv, strain_v, turb, ids_v, frac_v, ft, choose, W, lhs, vec,
     acc, disk, four, sendb,
     in_sem, out_sem, hs_sem, hr_sem, gs_sem, gr_sem, as_sem, ar_sem, row_sem, plane_sem,
 ):
@@ -185,6 +185,8 @@
     ]
     for copy in own:
         copy.start()
+    owners = pltpu.make_async_copy(owner_in, owner, in_sem.at[9])
+    owners.start()
 
     barrier = pltpu.get_barrier_semaphore()
 
@@ -318,6 +320,7 @@
         value = jnp.where(mine > 0, count * WIDTH, -AZIMUTHS) + lax.rem(lane8, WIDTH)
         return count + mine, jnp.where(here, value, place)
 
+    owners.wait()
     _, place = lax.fori_loop(
         0, SECTORS, sector, (jnp.int32(0), jnp.full((8, 128), -AZIMUTHS, jnp.int32))
     )
@@ -552,7 +555,6 @@
 def body(velocity, pressure, kinetic_energy, dissipation_rate, corner_ids, fractions, sector_owner):
     hbm = pl.BlockSpec(memory_space=pltpu.HBM)
     vmem = pl.BlockSpec(memory_space=pltpu.VMEM)
-    smem = pl.BlockSpec(memory_space=pltpu.SMEM)
     dma = pltpu.SemaphoreType.DMA
     shapes = (
         jax.ShapeDtypeStruct(velocity.shape, F32),
@@ -563,9 +565,10 @@
     results = pl.pallas_call(
         kernel,
         out_shape=shapes[:3] + (jax.ShapeDtypeStruct((PLANE * 8, 128), F32),),
-        in_specs=[hbm] * 6 + [smem, hbm],
+        in_specs=[hbm] * 8,
         out_specs=(hbm,) * 4,
         scratch_shapes=[
+            pltpu.SMEM((SECTORS,), jnp.int32),
             pltpu.VMEM((6, CELLS_S, CELLS_G, CELLS_R), F32),
             pltpu.VMEM((2, 6, 2, CELLS_G, CELLS_R), F32),
             pltpu.VMEM((6, CELLS_S, 24, CELLS_R), F32),
@@ -585,7 +588,7 @@
             pltpu.VMEM((48, 256), F32),
             pltpu.VMEM((512, 256), BF16),
             pltpu.VMEM((PLANE * 8, 128), F32),
-            dma((9,)),
+            dma((10,)),
             dma((7,)),
             dma((10,)),
             dma((10,)),

time: 29.7 us -> 29.1 us (0.980)
  Pallas kernels: 28.9 us -> 28.3 us
    pallas_call x1, Pallas kernels: 27.3 us -> 26.6 us  [body(): pl.pallas_call(kernel, out_shape=shapes[:3] + (jax.ShapeDtypeStruct((PLAN...]
where the time goes in v4:
time: 29.1 us; the launch traced here: 28.9 us
  Pallas kernels  28.3 us (97%)
  between operations  0.64 us (2%)
    pallas_call x1, Pallas kernels, body(): pl.pallas_call(kernel, out_shape=shapes[:3] + (jax.ShapeDtypeStruct((PLAN...  26.6 us
    pallas_call x1, Pallas kernels, body(): pl.pallas_call(place_results, out_shape=shapes, in_specs=[vmem] * 4, out_...  1.66 us

profile of v4, /device:TPU:1, one launch (start us, length us, event | category | flops | bytes accessed | tf_op | source)
XLA Modules:
  0.0 28.9 jit_solution(15813047585499689363)
XLA Ops:
  0.6 26.6 %shard_map.111 = (f32[3,4,8,256]{3,2,1,0:T(8,128)}, f32[4,8,256]{2,1,0:T(8,128)}, f32[4,8,256]{2,1,0:T(8,128)}, f32[256,128]{1,0:T(8,128)}) custom-call(f32[3,4,8,256]{3,2,1,0:T(8,128)} %vel.1, f32[4,8,256]{2,1,0:T(8,128)} %pre.1, f32[4,8,256]{2,1,0:T(8,128)} %kin.1, f32[4,8,256]{2,1,0:T(8,128)} %dis.1, s32[128,1024]{1,0:T(8,128)} %ids.1, ...), custom_call_target="tpu_custom_call" | custom-call | tf_op jit(solution)/shard_map/pallas_call | solution.py:565
  27.3 1.7 %shard_map.112 = (f32[3,4,8,256]{3,2,1,0:T(8,128)}, f32[4,8,256]{2,1,0:T(8,128)}, f32[4,8,256]{2,1,0:T(8,128)}, f32[1,768]{1,0:T(1,128)}) custom-call(f32[3,4,8,256]{3,2,1,0:T(8,128)} %get-tuple-element.8.nv, f32[4,8,256]{2,1,0:T(8,128)} %get-tuple-element.9.ne, f32[4,8,256]{2,1,0:T(8,128)} %get-tuple-element.10.nr, f32[256,128]{1,0:T(8,128)} %get-tuple-element.11.parts), custom_call_target="tpu_custom_call" | custom-call | tf_op jit(solution)/shard_map/pallas_call | solution.py:609

commit v5 on v4

--- a/solution.py
+++ b/solution.py
@@ -183,11 +183,7 @@
         pltpu.make_async_copy(kin, cells.at[4], in_sem.at[2]),
         pltpu.make_async_copy(dis, cells.at[5], in_sem.at[3]),
     ]
-    for copy in own:
-        copy.start()
     owners = pltpu.make_async_copy(owner_in, owner, in_sem.at[9])
-    owners.start()
-
     barrier = pltpu.get_barrier_semaphore()
 
     def plane_peer(across, step):
@@ -235,6 +231,8 @@
     for device in same_x + other_x + [across]:
         greet(device)
 
+    for copy in own:
+        copy.start()
     points = []
     for half in range(2):
         rows = pl.ds((half * RING + z) * GIRTH, GIRTH)
@@ -286,6 +284,7 @@
             pack[1, f, 2 * s : 2 * s + 2, :] = cells[f, s, 6:8, :]
     for side in (2, 3):
         each(side, sends, lambda copy: copy.start())
+    owners.start()
     for copy in points:
         copy.start()
     for device in other_x:
@@ -387,10 +386,6 @@
 
     for side in range(4):
         each(side, receives, lambda copy: copy.wait_recv())
-    for f in range(6):
-        for s in range(CELLS_S):
-            wide[f, s, 6:8, :] = edge[0, f, 2 * s : 2 * s + 2, :]
-            wide[f, s, 16:18, :] = edge[1, f, 2 * s : 2 * s + 2, :]
 
     def gather(i, s):
         return pltpu.make_async_remote_copy(
@@ -400,6 +395,9 @@
         )
 
     for s in range(CELLS_S):
+        for f in range(6):
+            wide[f, s, 6:8, :] = edge[0, f, 2 * s : 2 * s + 2, :]
+            wide[f, s, 16:18, :] = edge[1, f, 2 * s : 2 * s + 2, :]
         updated, strain = Layer(cells, above, wide, s).velocity()
         for c in range(3):
             nv[0, s, c] = updated[c]
@@ -458,7 +456,7 @@
             acc[c * TILES + n] = sums[c]
         return carry
 
-    lax.fori_loop(0, TILES, first_pass, 0, unroll=4)
+    lax.fori_loop(0, TILES, first_pass, 0, unroll=12)
 
     for i in range(1, RING):
         for s in range(CELLS_S):

time: 29.1 us -> 29.1 us (level)
  no operation moved by 1% of the time
where the time goes in v5:
time: 29.1 us; the launch traced here: 28.9 us
  Pallas kernels  28.3 us (97%)
  between operations  0.64 us (2%)
    pallas_call x1, Pallas kernels, body(): pl.pallas_call(kernel, out_shape=shapes[:3] + (jax.ShapeDtypeStruct((PLAN...  26.6 us
    pallas_call x1, Pallas kernels, body(): pl.pallas_call(place_results, out_shape=shapes, in_specs=[vmem] * 4, out_...  1.66 us

profile of v5, /device:TPU:1, one launch (start us, length us, event | category | flops | bytes accessed | tf_op | source)
XLA Modules:
  0.0 28.9 jit_solution(11226788218636619744)
XLA Ops:
  0.6 26.6 %shard_map.111 = (f32[3,4,8,256]{3,2,1,0:T(8,128)}, f32[4,8,256]{2,1,0:T(8,128)}, f32[4,8,256]{2,1,0:T(8,128)}, f32[256,128]{1,0:T(8,128)}) custom-call(f32[3,4,8,256]{3,2,1,0:T(8,128)} %vel.1, f32[4,8,256]{2,1,0:T(8,128)} %pre.1, f32[4,8,256]{2,1,0:T(8,128)} %kin.1, f32[4,8,256]{2,1,0:T(8,128)} %dis.1, s32[128,1024]{1,0:T(8,128)} %ids.1, ...), custom_call_target="tpu_custom_call" | custom-call | tf_op jit(solution)/shard_map/pallas_call | solution.py:563
  27.3 1.7 %shard_map.112 = (f32[3,4,8,256]{3,2,1,0:T(8,128)}, f32[4,8,256]{2,1,0:T(8,128)}, f32[4,8,256]{2,1,0:T(8,128)}, f32[1,768]{1,0:T(1,128)}) custom-call(f32[3,4,8,256]{3,2,1,0:T(8,128)} %get-tuple-element.8.nv, f32[4,8,256]{2,1,0:T(8,128)} %get-tuple-element.9.ne, f32[4,8,256]{2,1,0:T(8,128)} %get-tuple-element.10.nr, f32[256,128]{1,0:T(8,128)} %get-tuple-element.11.parts), custom_call_target="tpu_custom_call" | custom-call | tf_op jit(solution)/shard_map/pallas_call | solution.py:607
